TPU v7x, 32 devices: a whole 2x2x4 slice. The times are simulated.
32 devices in a mesh: groups: 2 (over y), tensor: 4 (over z), enc: 2 (over x), req: 2 (over core).
Axes of the slice: x: 2, y: 2, z: 4, core: 2. Of those that a mesh axis runs over, the one named last changes fastest.
Arguments:
- span_tokens: bfloat16 [8192, 1024], P(('groups', 'enc', 'req')), parts along dimension 0, may hold values from -6 to 6
- span_request: int32 [512, 1], P('groups'), parts along dimension 0, may hold values from 0 to 31; in each aligned block of 64 rows (0 to 63, 64 to 127, ...) at most 2 rows name the same one
- question_length: int32 [64], P(('groups', 'enc', 'req')), parts along dimension 0, may hold values from 8 to 32
- question_embed: bfloat16 [4096, 8192], P(('groups', 'enc', 'req'), 'tensor'), parts along dimension 0, may hold values from -6 to 6
- enc_up: bfloat16 [1024, 4096], P(None, 'tensor'), may hold values from -0.1875 to 0.1875
- enc_down: bfloat16 [4096, 1024], P('tensor'), may hold values from -0.09375 to 0.09375
- enc_gain: float32 [1024], replicated, may hold values from 0.1 to 1.9
- proj_weight: bfloat16 [1024, 8192], P(None, 'tensor'), may hold values from -0.75 to 0.75
- norm_gain: float32 [8192], replicated, may hold values from 0.1 to 1.9
- q_weight: bfloat16 [8192, 4096], P(None, 'tensor'), may hold values from -2 to 2
- k_weight: bfloat16 [8192, 512], P(None, 'tensor'), may hold values from -1 to 1
- v_weight: bfloat16 [8192, 512], P(None, 'tensor'), may hold values from -0.0625 to 0.0625
- o_weight: bfloat16 [4096, 8192], P(None, 'tensor'), may hold values from -0.375 to 0.375
Outputs:
- layer_out: bfloat16 [4096, 8192], P(('groups', 'enc', 'req'), 'tensor'), parts along dimension 0
There are 2 independent parts, one for each index of `groups`. A program takes and returns all parts, laid end to end along the dimension named above; an argument that names none is the same for every part. Nothing has to cross between parts.
Inputs may be any that keep to these rules, and one draw needn't show every extreme that they name: Span c belongs to request span_request[c, 0]; among the 64 spans of each aligned block of rows at most 2 belong to one request, and some block holds exactly 2 of one request. Every request has at least one span.
All inputs are finite; a program needn't handle non-finite values.
Results may differ from a plain program's by a relative error of at most 0.014.
Values may be sent and summed in bfloat16 or wider, within the bound.
A program may use at most 192 MiB of HBM per device.

v0:
```python
import math

import jax
import jax.numpy as jnp
from jax import lax
from jax.sharding import PartitionSpec as P

HQ = 32
KVH = 4
HD = 128
SPAN_LEN = 16
SLOT = 64
CAPR = 2


def rotate(values, positions):
    half_dim = values.shape[-1] // 2
    frequency = jnp.exp(
        jnp.arange(half_dim, dtype=jnp.float32) * (-2.0 * math.log(10000.0) / values.shape[-1])
    )
    angles = positions.astype(jnp.float32)[:, None] * frequency[None, :]
    cosine = jnp.cos(angles)[:, None, :]
    sines = jnp.sin(angles)[:, None, :]
    lower_half = values[..., :half_dim]
    upper_half = values[..., half_dim:]
    return jnp.concatenate(
        [lower_half * cosine - upper_half * sines, upper_half * cosine + lower_half * sines],
        axis=-1,
    )


def layer_norm(inputs, gain):
    center = inputs - jnp.mean(inputs, axis=-1, keepdims=True)
    spread = jnp.mean(center * center, axis=-1, keepdims=True)
    return center * lax.rsqrt(spread + 1e-05) * gain


def ffn_term(token_rows, enc_up, enc_down):
    enc_hidden = jax.nn.gelu(
        jnp.dot(token_rows, enc_up, preferred_element_type=jnp.float32), approximate=False
    ).astype(jnp.bfloat16)
    return jnp.dot(enc_hidden, enc_down, preferred_element_type=jnp.float32)


def pool_rows(token_rows, summed, enc_gain):
    encoded = layer_norm(token_rows.astype(jnp.float32) + summed, enc_gain)
    return jnp.mean(encoded.reshape(-1, SPAN_LEN, encoded.shape[-1]), axis=1).astype(jnp.bfloat16)


def shards(
    span_tokens,
    span_request,
    question_length,
    question_embed,
    enc_up,
    enc_down,
    enc_gain,
    proj_weight,
    norm_gain,
    q_weight,
    k_weight,
    v_weight,
    o_weight,
):
    tensor_count = lax.axis_size("tensor")
    tensor_place = lax.axis_index("tensor")
    owner_count = lax.axis_size(("enc", "req"))
    owner_place = lax.axis_index(("enc", "req"))
    share_rows = span_tokens.shape[0] // tensor_count
    kept_sums = lax.psum_scatter(
        ffn_term(span_tokens, enc_up, enc_down).astype(jnp.bfloat16),
        "tensor",
        scatter_dimension=0,
        tiled=True,
    ).astype(jnp.float32)
    kept_tokens = lax.dynamic_slice_in_dim(span_tokens, tensor_place * share_rows, share_rows, 0)
    pooled = lax.all_gather(
        pool_rows(kept_tokens, kept_sums, enc_gain), "tensor", axis=0, tiled=True
    )
    span_embed = jnp.dot(pooled, proj_weight, preferred_element_type=jnp.float32).astype(
        jnp.bfloat16
    )
    spans_here = span_embed.shape[0]
    columns = span_embed.shape[1]
    requests_here = question_length.shape[0]
    owners_of = span_request[:, 0]
    all_spans = owners_of.shape[0]
    slot_count = requests_here * CAPR
    my_requests = lax.dynamic_slice_in_dim(owners_of, owner_place * spans_here, spans_here, 0)
    index_here = jnp.arange(spans_here, dtype=jnp.int32)
    earlier = index_here[None, :] < index_here[:, None]
    same_request = my_requests[None, :] == my_requests[:, None]
    rank_here = jnp.sum(jnp.logical_and(same_request, earlier).astype(jnp.int32), axis=1)
    placement = (
        my_requests // requests_here * slot_count + my_requests % requests_here * CAPR + rank_here
    )
    spot_index = jnp.arange(owner_count * slot_count, dtype=jnp.int32)
    selector = (spot_index[:, None] == placement[None, :]).astype(jnp.bfloat16)
    outgoing = jnp.dot(selector, span_embed, preferred_element_type=jnp.float32).astype(
        jnp.bfloat16
    )
    outgoing = outgoing.reshape(owner_count, slot_count, columns)
    incoming = lax.all_to_all(outgoing, ("enc", "req"), split_axis=0, concat_axis=0, tiled=True)
    received = incoming.reshape(owner_count * slot_count, columns)
    local_requests = owner_place * requests_here + jnp.arange(requests_here, dtype=jnp.int32)
    member = (owners_of[None, :] == local_requests[:, None]).astype(jnp.int32)
    arrive = jnp.cumsum(member, axis=1) - member
    counts = jnp.sum(member, axis=1)
    blocked = member.reshape(requests_here, owner_count, spans_here)
    within = (jnp.cumsum(blocked, axis=2) - blocked).reshape(requests_here, all_spans)
    sender = jnp.arange(all_spans, dtype=jnp.int32) // spans_here
    source = (
        sender[None, :] * slot_count
        + jnp.arange(requests_here, dtype=jnp.int32)[:, None] * CAPR
        + within
    )
    positions = jnp.arange(SLOT, dtype=jnp.int32)
    matches = member[:, :, None] * (arrive[:, :, None] == positions[None, None, :]).astype(
        jnp.int32
    )
    row_source = jnp.sum(matches * source[:, :, None], axis=1)
    is_span = positions[None, :] < counts[:, None]
    live = positions[None, :] < (counts + question_length)[:, None]
    is_question = jnp.logical_and(jnp.logical_not(is_span), live)
    question_rows = jnp.arange(requests_here, dtype=jnp.int32)[:, None] * SLOT + jnp.clip(
        positions[None, :] - counts[:, None], 0, SLOT - 1
    )
    from_spans = jnp.take(received, row_source.reshape(-1), axis=0)
    from_questions = jnp.take(question_embed, question_rows.reshape(-1), axis=0)
    zero_rows = jnp.zeros_like(from_spans)
    decoder_in = jnp.where(
        is_span.reshape(-1, 1),
        from_spans,
        jnp.where(is_question.reshape(-1, 1), from_questions, zero_rows),
    )
    full_rows = lax.all_gather(decoder_in, "tensor", axis=1, tiled=True)
    full32 = full_rows.astype(jnp.float32)
    normed = (
        full32 * lax.rsqrt(jnp.mean(full32 * full32, axis=-1, keepdims=True) + 1e-05) * norm_gain
    ).astype(jnp.bfloat16)
    query_raw = jnp.dot(normed, q_weight, preferred_element_type=jnp.float32)
    key_part = jnp.dot(normed, k_weight, preferred_element_type=jnp.float32).astype(jnp.bfloat16)
    value_part = jnp.dot(normed, v_weight, preferred_element_type=jnp.float32).astype(jnp.bfloat16)
    stacked = jnp.stack([key_part, value_part], axis=0)
    gathered = lax.all_gather(stacked, "tensor", axis=2, tiled=True)
    row_count = decoder_in.shape[0]
    key_all = gathered[0].reshape(row_count, HD, KVH)
    value_all = gathered[1].reshape(row_count, HD, KVH)
    heads_here = q_weight.shape[1] // HD
    shared_head = tensor_place * heads_here // (HQ // KVH)
    key_head = lax.dynamic_slice_in_dim(key_all, shared_head, 1, 2)[:, :, 0]
    value_head = lax.dynamic_slice_in_dim(value_all, shared_head, 1, 2)[:, :, 0]
    queries = rotate(query_raw.reshape(requests_here, SLOT, heads_here, HD), positions).astype(
        jnp.bfloat16
    )
    keys = rotate(key_head.astype(jnp.float32).reshape(requests_here, SLOT, 1, HD), positions)[
        :, :, 0, :
    ].astype(jnp.bfloat16)
    values = value_head.reshape(requests_here, SLOT, HD)
    scores = jnp.einsum(
        "rphd,rqd->rhpq", queries, keys, preferred_element_type=jnp.float32
    ) * HD ** (-0.5)
    allowed = jnp.logical_and(
        (positions[:, None] >= positions[None, :])[None, None, :, :], live[:, None, None, :]
    )
    scores = jnp.where(allowed, scores, -jnp.inf)
    probs = jax.nn.softmax(scores, axis=-1).astype(jnp.bfloat16)
    context = jnp.einsum(
        "rhpq,rqd->rphd", probs, values, preferred_element_type=jnp.float32
    ).astype(jnp.bfloat16)
    context = context.reshape(row_count, heads_here * HD)
    mixed = jnp.dot(
        lax.all_gather(context, "tensor", axis=1, tiled=True),
        o_weight,
        preferred_element_type=jnp.float32,
    )
    summed = decoder_in.astype(jnp.float32) + mixed
    return jnp.where(live.reshape(-1, 1), summed, jnp.zeros_like(summed)).astype(jnp.bfloat16)


def solution(mesh):
    return jax.shard_map(
        shards,
        mesh=mesh,
        in_specs=(
            P(("groups", "enc", "req"), None),
            P("groups", None),
            P(("groups", "enc", "req")),
            P(("groups", "enc", "req"), "tensor"),
            P(None, "tensor"),
            P("tensor", None),
            P(),
            P(None, "tensor"),
            P(),
            P(None, "tensor"),
            P(None, "tensor"),
            P(None, "tensor"),
            P(None, "tensor"),
        ),
        out_specs=P(("groups", "enc", "req"), "tensor"),
        check_vma=False,
    )
```

profile of v0, /device:TPU:0, one launch (start us, length us, event | category | flops | bytes accessed | tf_op | source)
XLA Modules:
  0.0 408.1 jit_solution(9781169069994422103)
XLA Ops:
  6.5 1.6 copy-done
  8.1 15.5 %fusion.16 = bf16[1024,1024]{1,0:T(8,128)(2,1)} fusion(bf16[1024,1024]{1,0:T(8,128)(2,1)S(1)} %copy-done, bf16[1024,1024]{1,0:T(8,128)(2,1)} %param.13, bf16[1024,1024]{1,0:T(8,128)(2,1)} %param.17), kind=kOutput, calls=%fused_computation.37 | convolution fusion | flops 4364173312 | bytes 8388608 | tf_op jit(solution)/shard_map/dot_general | solution.py:42
  28.2 3.3 gather_fusion.1
  31.8 38.5 %reduce-scatter.2.cloned.1.call-done = bf16[256,1024]{1,0:T(8,128)(2,1)} async-done(((bf16[1024,1024]{1,0:T(8,128)(2,1)}), bf16[256,1024]{1,0:T(8,128)(2,1)}) %reduce-scatter.2.cloned.1.call-update) | async-done | bytes 524304 | tf_op jit(solution)/shard_map/reduce_scatter | solution.py:70
  70.3 1.4 fusion.31
  71.7 1.5 multiply_reduce_fusion
  73.3 1.6 bitcast_reduce_fusion
  74.9 13.4 %all_gather.12 = bf16[64,1024]{1,0:T(8,128)(2,1)S(1)} all-gather(bf16[16,1024]{1,0:T(8,128)(2,1)S(1)} %multiply_convert_fusion), channel_id=1, replica_groups=mesh['groups'=2,'tensor'=4,'enc'=2,'req'=2] {'tensor'}, dimensions={0}, use_global_device_ids=true | all-gather | bytes 163840 | tf_op jit(solution)/shard_map/all_gather | solution.py:77
  88.3 3.9 convolution_convert_fusion
  92.1 3.4 all-to-all-start
  95.6 5.9 %all-to-all-done = bf16[4,16,2048]{2,1,0:T(8,128)(2,1)S(1)} async-done(((bf16[4,16,2048]{2,1,0:T(8,128)(2,1)}), bf16[4,16,2048]{2,1,0:T(8,128)(2,1)S(1)}, u32[]{:S(2)}, u32[]{:S(2)}) %all-to-all-start) | async-done | bytes 262176 | tf_op jit(solution)/shard_map/all_to_all | solution.py:103
  101.6 3.3 gather_fusion
  104.9 3.0 select_select_fusion
  108.5 147.5 %all-gather.4.cloned.1.call-done = bf16[512,8192]{1,0:T(8,128)(2,1)} async-done(((bf16[512,2048]{1,0:T(8,128)(2,1)}), bf16[512,8192]{1,0:T(8,128)(2,1)}) %all-gather.4.cloned.1.call-update) | async-done | bytes 8388624 | tf_op jit(solution)/shard_map/all_gather | solution.py:136
  256.1 5.3 %fusion.1 = f32[512]{0:T(512)S(1)} fusion(bf16[512,8192]{1,0:T(8,128)(2,1)} %all-gather.4.cloned.1.call-done), kind=kLoop, calls=%fused_computation.5 | loop fusion | flops 12582400 | bytes 8390656 | tf_op jit(solution)/shard_map/reduce_sum | solution.py:139
  261.8 2.5 fusion.22
  264.3 2.4 fusion.21
  267.7 14.5 %convolution_bitcast_fusion = f32[64,8,8,128]{3,1,2,0:T(8,128)S(1)} fusion(bf16[8192,1024]{1,0:T(8,128)(2,1)} %param.22, bf16[512,8192]{1,0:T(8,128)(2,1)} %all-gather.4.cloned.1.call-done, f32[8192]{0:T(1024)S(1)} %copy-done.9, f32[512]{0:T(512)S(1)} %add_rsqrt_fusion), kind=kOutput, calls=%fused_computation.39 | convolution fusion | flops 8606711808 | bytes 27297792 | tf_op jit(solution)/shard_map/dot_general | solution.py:141
  283.4 1.8 subtract_convert_fusion
  285.3 10.7 %all-gather.6.cloned.1.call-done = bf16[2,512,512]{2,1,0:T(8,128)(2,1)} async-done(((bf16[2,512,128]{2,1,0:T(8,128)(2,1)}), bf16[2,512,512]{2,1,0:T(8,128)(2,1)}) %all-gather.6.cloned.1.call-update) | async-done | bytes 1048592 | tf_op jit(solution)/shard_map/all_gather | solution.py:145
  299.1 4.1 %fusion.86 = (f32[8,8,64]{2,1,0:T(8,128)S(1)}, f32[8,8,64,64]{2,3,1,0:T(8,128)}) fusion(pred[8,64,64]{1,2,0:T(8,128)(4,1)S(1)} %broadcast_and_fusion, bf16[8,64,8,64]{3,1,2,0:T(8,128)(2,1)} %get-tuple-element.6, bf16[8,64,8,64]{3,1,2,0:T(8,128)(2,1)S(1)} %get-tuple-element.5, bf16[8,64,1,64]{3,1,0,2:T(8,128)(2,1)S(1)} %get-tuple-element.12, ...), kind=kOutput, calls=%fused_computation.157 | convolution fusion | flops 70516800 | bytes 2277376 | tf_op jit(solution)/shard_map/sub | solution.py:167
  303.2 2.1 fusion.20
  307.3 79.2 %all-gather.8.cloned.1.call-done = bf16[512,4096]{1,0:T(8,128)(2,1)} async-done(((bf16[512,1024]{1,0:T(8,128)(2,1)}), bf16[512,4096]{1,0:T(8,128)(2,1)}) %all-gather.8.cloned.1.call-update) | async-done | bytes 4194320 | tf_op jit(solution)/shard_map/all_gather | solution.py:173
  386.5 15.0 %select_convert_fusion = bf16[512,2048]{1,0:T(8,128)(2,1)} fusion(bf16[512,2048]{1,0:T(8,128)(2,1)} %select_select_fusion, bf16[512,4096]{1,0:T(8,128)(2,1)} %all-gather.8.cloned.1.call-done, bf16[4096,2048]{1,0:T(8,128)(2,1)} %param.25, pred[512]{0:T(512)(128)(4,1)S(1)} %lt.124), kind=kOutput, calls=%fused_computation.12 | convolution fusion | flops 8594128896 | bytes 25166336 | tf_op jit(solution)/shard_map/dot_general | solution.py:172
  (92 shorter events, 13.2 us)
Async XLA Ops:
  6.5 1.6 copy-start
  6.5 17.6 %copy-start.5 = (s32[256,1]{0,1:T(1,128)S(1)}, s32[256,1]{0,1:T(1,128)}, u32[]{:S(2)}) copy-start(s32[256,1]{0,1:T(1,128)} %param.14) | copy-start | bytes 3076
  6.5 21.3 %copy-start.10 = (s32[8]{0:T(128)S(1)}, s32[8]{0:T(128)}, u32[]{:S(2)}) copy-start(s32[8]{0:T(128)} %param.15) | copy-start | bytes 100
  6.5 63.8 %reduce-scatter.2.cloned.1.call-start = ((), (), s32[]{:S(2)}) async-start(), calls=%async_computation.2 | async-start | bytes 2621440 | tf_op jit(solution)/shard_map/reduce_scatter | solution.py:70
  23.6 4.6 %copy-start.2 = (bf16[512,2048]{1,0:T(8,128)(2,1)S(1)}, bf16[512,2048]{1,0:T(8,128)(2,1)}, u32[]{:S(2)}) copy-start(bf16[512,2048]{1,0:T(8,128)(2,1)} %param.16) | copy-start | bytes 6291460
  28.2 45.1 %copy-start.6 = (f32[1024]{0:T(1024)S(1)}, f32[1024]{0:T(1024)}, u32[]{:S(2)}) copy-start(f32[1024]{0:T(1024)} %param.19) | copy-start | bytes 12292
  92.1 9.4 %all-to-all-start = ((bf16[4,16,2048]{2,1,0:T(8,128)(2,1)}), bf16[4,16,2048]{2,1,0:T(8,128)(2,1)S(1)}, u32[]{:S(2)}, u32[]{:S(2)}) async-start(bf16[4,16,2048]{2,1,0:T(8,128)(2,1)} %bitcast.5), calls=%async_computation.1 | async-start | bytes 524288 | tf_op jit(solution)/shard_map/all_to_all | solution.py:103
  95.6 160.5 %all-gather.4.cloned.1.call-start = ((), (), s32[]{:S(2)}) async-start(), calls=%async_computation.3 | async-start | bytes 10485760 | tf_op jit(solution)/shard_map/all_gather | solution.py:136
  101.6 3.3 copy-start.3
  107.9 153.5 %copy-start.7 = (bf16[8192,128]{1,0:T(8,128)(2,1)S(1)}, bf16[8192,128]{1,0:T(8,128)(2,1)}, u32[]{:S(2)}) copy-start(bf16[8192,128]{1,0:T(8,128)(2,1)} %param.24) | copy-start | bytes 6291460
  107.9 188.1 %all-gather.6.cloned.1.call-start = ((), (), s32[]{:S(2)}) async-start(), calls=%async_computation.4 | async-start | bytes 1310720 | tf_op jit(solution)/shard_map/all_gather | solution.py:145
  108.4 153.0 %copy-start.9 = (f32[8192]{0:T(1024)S(1)}, f32[8192]{0:T(1024)}, u32[]{:S(2)}) copy-start(f32[8192]{0:T(1024)} %param.21) | copy-start | bytes 98308
  256.1 5.8 %copy-start.4 = (bf16[512,8192]{1,0:T(8,128)(2,1)S(1)}, bf16[512,8192]{1,0:T(8,128)(2,1)}, u32[]{:S(2)}) copy-start(bf16[512,8192]{1,0:T(8,128)(2,1)} %all-gather.4.cloned.1.call-done) | copy-start | bytes 25165828
  261.8 2.5 copy-start.8
  267.5 119.0 %all-gather.8.cloned.1.call-start = ((), (), s32[]{:S(2)}) async-start(), calls=%async_computation.5 | async-start | bytes 5242880 | tf_op jit(solution)/shard_map/all_gather | solution.py:173
  386.5 15.0 %copy-start.1 = (bf16[1024,1024]{1,0:T(8,128)(2,1)S(1)}, bf16[1024,1024]{1,0:T(8,128)(2,1)}, u32[]{:S(2)}) copy-start(bf16[1024,1024]{1,0:T(8,128)(2,1)} %param.18) | copy-start | bytes 6291460
Sparse Core Ops, SparseCore 0:
  23.7 46.5 reduce-scatter.1
  108.0 148.0 all-gather.3
  267.6 28.3 all-gather.5
  307.4 79.0 all-gather.7
where the time goes:
time: 409 us; the launch traced here: 408 us
  waiting for transfers between devices  282 us (69%)
  matrix products  59.9 us (15%)
  other arithmetic  19.3 us (5%)
  local copies, waits for them, and re-layouts  16.2 us (4%)
  blocking collectives  13.4 us (3%)
  between operations  13.4 us (3%)
    all_gather x1, waiting for transfers between devices, shards(): full_rows = lax.all_gather(decoder_in, 'tensor', axis=1, tiled=True)  148 us
    all_gather x1, waiting for transfers between devices, shards(): lax.all_gather(context, 'tensor', axis=1, tiled=True)  79.2 us
    reduce_scatter x1, waiting for transfers between devices, shards(): lax.psum_scatter(ffn_term(span_tokens, enc_up, enc_down).astype(jnp.bfloa...  38.5 us
    dot_general x1, matrix products, ffn_term(): return jnp.dot(enc_hidden, enc_down, preferred_element_type=jnp.float32)  15.5 us
    dot_general x1, matrix products, shards(): jnp.dot(lax.all_gather(context, 'tensor', axis=1, tiled=True), o_weight,...  15 us
    dot_general x1, matrix products, shards(): query_raw = jnp.dot(normed, q_weight, preferred_element_type=jnp.float32)  14.5 us
    all_gather x1, blocking collectives, shards(): lax.all_gather(pool_rows(kept_tokens, kept_sums, enc_gain), 'tensor', axi...  13.4 us
    all_gather x1, waiting for transfers between devices, shards(): gathered = lax.all_gather(stacked, 'tensor', axis=2, tiled=True)  10.7 us
  transfers between devices with their start and end apart: 5, of which 5 were waited for; matrix products, arithmetic and copies ran while one was open for 6% of the time, Pallas kernels for 0%

commit v1 on v0

v1 whole, which is shorter than its diff:
```python
import math

import jax
import jax.numpy as jnp
from jax import lax
from jax.sharding import PartitionSpec as P

HQ = 32
KVH = 4
HD = 128
SPAN_LEN = 16
SLOT = 64
CAPR = 2
QUESTION_MAX = 32


def rope_tables(positions):
    half_dim = HD // 2
    frequency = jnp.exp(
        jnp.arange(half_dim, dtype=jnp.float32) * (-2.0 * math.log(10000.0) / HD)
    )
    angles = positions.astype(jnp.float32)[..., None] * frequency
    return jnp.cos(angles), jnp.sin(angles)


def rotate(values, cosine, sines):
    half_dim = values.shape[-1] // 2
    lower_half = values[..., :half_dim]
    upper_half = values[..., half_dim:]
    return jnp.concatenate(
        [lower_half * cosine - upper_half * sines, upper_half * cosine + lower_half * sines],
        axis=-1,
    )


def layer_norm(inputs, gain):
    center = inputs - jnp.mean(inputs, axis=-1, keepdims=True)
    spread = jnp.mean(center * center, axis=-1, keepdims=True)
    return center * lax.rsqrt(spread + 1e-05) * gain


def ffn_term(token_rows, enc_up, enc_down):
    enc_hidden = jax.nn.gelu(
        jnp.dot(token_rows, enc_up, preferred_element_type=jnp.float32), approximate=False
    ).astype(jnp.bfloat16)
    return jnp.dot(enc_hidden, enc_down, preferred_element_type=jnp.float32)


def pool_rows(token_rows, summed, enc_gain):
    encoded = layer_norm(token_rows.astype(jnp.float32) + summed, enc_gain)
    return jnp.mean(encoded.reshape(-1, SPAN_LEN, encoded.shape[-1]), axis=1).astype(jnp.bfloat16)


def rms(rows, gain):
    wide = rows.astype(jnp.float32)
    return (
        wide * lax.rsqrt(jnp.mean(wide * wide, axis=-1, keepdims=True) + 1e-05) * gain
    ).astype(jnp.bfloat16)


def shards(
    span_tokens,
    span_request,
    question_length,
    question_embed,
    enc_up,
    enc_down,
    enc_gain,
    proj_weight,
    norm_gain,
    q_weight,
    k_weight,
    v_weight,
    o_weight,
):
    tensor_count = lax.axis_size("tensor")
    tensor_place = lax.axis_index("tensor")
    owner_count = lax.axis_size(("enc", "req"))
    owner_place = lax.axis_index(("enc", "req"))
    requests_here = question_length.shape[0]
    columns = question_embed.shape[1]
    span_room = CAPR * owner_count
    room = min(SLOT, span_room + QUESTION_MAX)

    questions = question_embed.reshape(requests_here, SLOT, columns)[:, :QUESTION_MAX]
    questions = questions.reshape(-1, columns)
    question_full = lax.all_gather(questions, "tensor", axis=1, tiled=True)

    share_rows = span_tokens.shape[0] // tensor_count
    kept_sums = lax.psum_scatter(
        ffn_term(span_tokens, enc_up, enc_down).astype(jnp.bfloat16),
        "tensor",
        scatter_dimension=0,
        tiled=True,
    ).astype(jnp.float32)
    kept_tokens = lax.dynamic_slice_in_dim(span_tokens, tensor_place * share_rows, share_rows, 0)
    pooled = lax.all_gather(
        pool_rows(kept_tokens, kept_sums, enc_gain), "tensor", axis=0, tiled=True
    )

    spans_here = pooled.shape[0]
    owners_of = span_request[:, 0]
    all_spans = owners_of.shape[0]
    blocks = owners_of.reshape(owner_count, spans_here)
    index_here = jnp.arange(spans_here, dtype=jnp.int32)
    earlier = index_here[None, :] < index_here[:, None]
    my_spans = lax.dynamic_slice_in_dim(blocks, owner_place, 1, 0)[0]
    same_request = my_spans[None, :] == my_spans[:, None]
    rank_here = jnp.sum(jnp.logical_and(same_request, earlier).astype(jnp.int32), axis=1)
    slot_count = requests_here * CAPR
    placement = my_spans * CAPR + rank_here
    spot_index = jnp.arange(owner_count * slot_count, dtype=jnp.int32)
    selector = (spot_index[:, None] == placement[None, :]).astype(jnp.bfloat16)
    placed = jnp.dot(selector, pooled, preferred_element_type=jnp.float32).astype(jnp.bfloat16)
    incoming = lax.all_to_all(
        placed.reshape(owner_count, slot_count, -1),
        ("enc", "req"),
        split_axis=0,
        concat_axis=0,
        tiled=True,
    )
    incoming = incoming.reshape(owner_count, requests_here, CAPR, -1)
    incoming = jnp.swapaxes(incoming, 0, 1).reshape(requests_here * span_room, -1)
    span_rows = jnp.dot(incoming, proj_weight, preferred_element_type=jnp.float32).astype(
        jnp.bfloat16
    )
    span_full = lax.all_gather(span_rows, "tensor", axis=1, tiled=True)

    requests_all = requests_here * owner_count
    exact = all_spans == requests_all * span_room
    local_requests = owner_place * requests_here + jnp.arange(requests_here, dtype=jnp.int32)
    if exact:
        slot_positions = jnp.broadcast_to(
            jnp.arange(room, dtype=jnp.int32)[None, :], (requests_here, room)
        )
        counts = jnp.full((requests_here,), span_room, jnp.int32)
        live = slot_positions < (counts + question_length)[:, None]
    else:
        per_block = jnp.sum(
            (blocks[None, :, :] == local_requests[:, None, None]).astype(jnp.int32), axis=2
        )
        counts = jnp.sum(per_block, axis=1)
        before = jnp.cumsum(per_block, axis=1) - per_block
        rank = jnp.arange(CAPR, dtype=jnp.int32)
        span_positions = (before[:, :, None] + rank[None, None, :]).reshape(requests_here, -1)
        span_live = (rank[None, None, :] < per_block[:, :, None]).reshape(requests_here, -1)
        turn = jnp.arange(QUESTION_MAX, dtype=jnp.int32)
        question_positions = counts[:, None] + turn[None, :]
        question_live = turn[None, :] < question_length[:, None]
        slot_positions = jnp.concatenate([span_positions, question_positions], axis=1)
        live = jnp.concatenate([span_live, question_live], axis=1)

    kv_columns = k_weight.shape[1]
    entries = kv_columns // KVH
    kv_weight = jnp.stack(
        [k_weight.reshape(-1, entries, KVH), v_weight.reshape(-1, entries, KVH)], axis=1
    )
    kv_weight = jnp.transpose(kv_weight, (0, 3, 1, 2)).reshape(k_weight.shape[0], -1)
    heads_here = q_weight.shape[1] // HD

    def project(rows, slots):
        normed = rms(rows, norm_gain)
        kv = jnp.dot(normed, kv_weight, preferred_element_type=jnp.float32).astype(jnp.bfloat16)
        query = jnp.dot(normed, q_weight, preferred_element_type=jnp.float32)
        cosine, sines = rope_tables(slots)
        query = rotate(
            query.reshape(requests_here, -1, heads_here, HD),
            cosine[:, :, None, :],
            sines[:, :, None, :],
        ).astype(jnp.bfloat16)
        return query, kv.reshape(requests_here, -1, 2 * kv_columns)

    question_queries, question_kv = project(question_full, slot_positions[:, span_room:])
    span_queries, span_kv = project(span_full, slot_positions[:, :span_room])
    queries = jnp.concatenate([span_queries, question_queries], axis=1)
    kv = jnp.concatenate([span_kv, question_kv], axis=1)
    slots = kv.shape[1]
    if tensor_count == KVH:
        kv = kv.reshape(requests_here * slots, KVH, 2 * entries)
        kv = lax.all_to_all(
            jnp.swapaxes(kv, 0, 1), "tensor", split_axis=0, concat_axis=0, tiled=True
        )
        kv = kv.reshape(tensor_count, requests_here, slots, 2, entries)
    else:
        kv = lax.all_gather(kv, "tensor", axis=0, tiled=False)
        kv = kv.reshape(tensor_count, requests_here, slots, KVH, 2, entries)
        shared_head = tensor_place * heads_here // (HQ // KVH)
        kv = lax.dynamic_slice_in_dim(kv, shared_head, 1, 3)[:, :, :, 0]
    kv = jnp.transpose(kv, (3, 1, 2, 0, 4)).reshape(2, requests_here, slots, HD)
    cosine, sines = rope_tables(slot_positions)
    keys = rotate(kv[0].astype(jnp.float32), cosine, sines).astype(jnp.bfloat16)
    values = kv[1]

    local_rows = jnp.concatenate(
        [
            span_rows.reshape(requests_here, span_room, columns),
            questions.reshape(requests_here, QUESTION_MAX, columns),
        ],
        axis=1,
    )
    if not exact:
        at = jnp.arange(room, dtype=jnp.int32)
        order = jnp.logical_and(
            at[None, :, None] == slot_positions[:, None, :], live[:, None, :]
        ).astype(jnp.bfloat16)
        local_rows = jnp.einsum(
            "rps,rsc->rpc", order, local_rows, preferred_element_type=jnp.float32
        ).astype(jnp.bfloat16)
    live_rows = jnp.arange(room, dtype=jnp.int32)[None, :] < (counts + question_length)[:, None]

    def attend(low, high):
        scores = jnp.einsum(
            "rphd,rqd->rhpq",
            queries[low:high],
            keys[low:high],
            preferred_element_type=jnp.float32,
        ) * HD ** (-0.5)
        spots = slot_positions[low:high]
        allowed = jnp.logical_and(
            spots[:, :, None] >= spots[:, None, :], live[low:high][:, None, :]
        )
        scores = jnp.where(allowed[:, None], scores, -1e30)
        probs = jax.nn.softmax(scores, axis=-1).astype(jnp.bfloat16)
        context = jnp.einsum(
            "rhpq,rqd->rphd", probs, values[low:high], preferred_element_type=jnp.float32
        ).astype(jnp.bfloat16)
        context = context.reshape(high - low, slots, heads_here * HD)
        if not exact:
            context = jnp.einsum(
                "rps,rsc->rpc", order[low:high], context, preferred_element_type=jnp.float32
            ).astype(jnp.bfloat16)
        return lax.all_gather(
            context.reshape((high - low) * room, -1), "tensor", axis=1, tiled=True
        )

    half = requests_here // 2
    outs = []
    for low, high in ((0, half), (half, requests_here)):
        mixed = jnp.dot(attend(low, high), o_weight, preferred_element_type=jnp.float32)
        mixed = mixed.reshape(high - low, room, columns)
        summed = local_rows[low:high].astype(jnp.float32) + mixed
        outs.append(
            jnp.where(live_rows[low:high][:, :, None], summed, jnp.zeros_like(summed)).astype(
                jnp.bfloat16
            )
        )
    out = jnp.concatenate(outs, axis=0)
    return jnp.pad(out, ((0, 0), (0, SLOT - room), (0, 0))).reshape(-1, columns)


def solution(mesh):
    return jax.shard_map(
        shards,
        mesh=mesh,
        in_specs=(
            P(("groups", "enc", "req"), None),
            P("groups", None),
            P(("groups", "enc", "req")),
            P(("groups", "enc", "req"), "tensor"),
            P(None, "tensor"),
            P("tensor", None),
            P(),
            P(None, "tensor"),
            P(),
            P(None, "tensor"),
            P(None, "tensor"),
            P(None, "tensor"),
            P(None, "tensor"),
        ),
        out_specs=P(("groups", "enc", "req"), "tensor"),
        check_vma=False,
    )
```

time: 409 us -> 319 us (0.78)
  waiting for transfers between devices: 282 us -> 173 us
  local copies, waits for them, and re-layouts: 16.2 us -> 23.9 us
  blocking collectives: 13.4 us -> 20.5 us
  matrix products: 59.9 us -> 65.1 us
    all_gather x3 -> x4, waiting for transfers between devices: 237 us -> 128 us  [the longest x1 69.4 us: shards(): question_full = lax.all_gather(questions, 'tensor', axis=1, tiled=True)]
    dot_general x6 -> x12, matrix products: 40.4 us -> 48.4 us  [the longest x2 18.9 us: project(): query = jnp.dot(normed, q_weight, preferred_element_type=jnp.float32)]
    all_to_all x0 -> x1, blocking collectives: none -> 7.15 us  [shards(): lax.all_to_all(placed.reshape(owner_count, slot_count, -1), ('enc', 'req'...]
    gather x2 -> x0, local copies, waits for them, and re-layouts: 6.62 us -> none  [the longest x1 3.34 us: shards(): from_spans = jnp.take(received, row_source.reshape(-1), axis=0)]
    reduce_scatter x1, waiting for transfers between devices: 38.5 us -> 45 us  [shards(): lax.psum_scatter(ffn_term(span_tokens, enc_up, enc_down).astype(jnp.bfloa...]
    all_to_all x1, waiting for transfers between devices: 5.94 us -> 0.01 us  [shards(): lax.all_to_all(jnp.swapaxes(kv, 0, 1), 'tensor', split_axis=0, concat_axi...]
    unnamed x26 -> x32, local copies, waits for them, and re-layouts: 4.53 us -> 10.3 us
    transpose x0 -> x1, other arithmetic: none -> 5.38 us  [shards(): jnp.transpose(kv_weight, (0, 3, 1, 2)).reshape(k_weight.shape[0], -1)]
  transfers between devices with their start and end apart: 5 -> 6, of which waited for: 5 -> 5; matrix products, arithmetic and copies ran while one was open for 6% -> 19% of each run, Pallas kernels for 0% -> 0%
where the time goes in v1:
time: 319 us
  waiting for transfers between devices  173 us (54%)
  matrix products  65.1 us (20%)
  local copies, waits for them, and re-layouts  23.9 us (7%)
  blocking collectives  20.5 us (6%)
  other arithmetic  19.4 us (6%)
  between operations  13.6 us (4%)
  starting transfers between devices  3.53 us (1%)
    all_gather x1, waiting for transfers between devices, shards(): question_full = lax.all_gather(questions, 'tensor', axis=1, tiled=True)  69.4 us
    all_gather x2, waiting for transfers between devices, attend(): lax.all_gather(context.reshape((high - low) * room, -1), 'tensor', axis=1...  54.8 us
    reduce_scatter x1, waiting for transfers between devices, shards(): lax.psum_scatter(ffn_term(span_tokens, enc_up, enc_down).astype(jnp.bfloa...  45 us
    dot_general x2, matrix products, project(): query = jnp.dot(normed, q_weight, preferred_element_type=jnp.float32)  18.9 us
    dot_general x2, matrix products, shards(): jnp.dot(attend(low, high), o_weight, preferred_element_type=jnp.float32)  17.9 us
    dot_general x1, matrix products, ffn_term(): return jnp.dot(enc_hidden, enc_down, preferred_element_type=jnp.float32)  15.4 us
    all_gather x1, blocking collectives, shards(): lax.all_gather(pool_rows(kept_tokens, kept_sums, enc_gain), 'tensor', axi...  13.4 us
    unnamed x32, local copies, waits for them, and re-layouts  10.3 us
  transfers between devices with their start and end apart: 6, of which 5 were waited for; matrix products, arithmetic and copies ran while one was open for 19% of the time, Pallas kernels for 0%

profile of v1, /device:TPU:0, one launch (start us, length us, event | category | flops | bytes accessed | tf_op | source)
XLA Modules:
  0.0 318.7 jit_solution(13530906133650773894)
XLA Ops:
  8.1 15.4 %fusion.23 = bf16[1024,1024]{1,0:T(8,128)(2,1)} fusion(bf16[1024,1024]{1,0:T(8,128)(2,1)S(1)} %copy-done, bf16[1024,1024]{1,0:T(8,128)(2,1)} %param.13, bf16[1024,1024]{1,0:T(8,128)(2,1)} %param.17), kind=kOutput, calls=%fused_computation.38 | convolution fusion | flops 4364173312 | bytes 8388608 | tf_op jit(solution)/shard_map/dot_general | solution.py:46
  25.2 45.0 %reduce-scatter.2.cloned.1.call-done = bf16[256,1024]{1,0:T(8,128)(2,1)} async-done(((bf16[1024,1024]{1,0:T(8,128)(2,1)}), bf16[256,1024]{1,0:T(8,128)(2,1)}) %reduce-scatter.2.cloned.1.call-update) | async-done | bytes 524304 | tf_op jit(solution)/shard_map/reduce_scatter | solution.py:90
  73.2 1.6 bitcast_reduce_fusion
  74.8 13.4 %all_gather.15 = bf16[64,1024]{1,0:T(8,128)(2,1)S(1)} all-gather(bf16[16,1024]{1,0:T(8,128)(2,1)S(1)} %multiply_convert_fusion), channel_id=1, replica_groups=mesh['groups'=2,'tensor'=4,'enc'=2,'req'=2] {'tensor'}, dimensions={0}, use_global_device_ids=true | all-gather | bytes 163840 | tf_op jit(solution)/shard_map/all_gather | solution.py:97
  88.4 7.2 %all_to_all.10 = bf16[4,16,1024]{2,1,0:T(8,128)(2,1)S(1)} all-to-all(bf16[4,16,1024]{2,1,0:T(8,128)(2,1)S(1)} %bitcast.129), channel_id=1, replica_groups=mesh['groups'=2,'tensor'=4,'enc'=2,'req'=2] {'enc','req'}, dimensions={0} | all-to-all | bytes 262144 | tf_op jit(solution)/shard_map/all_to_all | solution.py:115
  95.8 3.8 %convolution_convert_fusion = bf16[64,2048]{1,0:T(8,128)(2,1)} fusion(bf16[64,1024]{1,0:T(8,128)(2,1)S(1)} %reshape.132, bf16[1024,2048]{1,0:T(8,128)(2,1)} %param.20), kind=kOutput, calls=%fused_computation.32 | convolution fusion | flops 268566528 | bytes 4587520 | tf_op jit(solution)/shard_map/dot_general | solution.py:124
  99.6 2.4 slice.111
  102.1 2.9 copy.63
  105.0 2.2 stack_reshape.6
  107.2 2.9 copy.64
  110.1 2.2 stack_reshape.7
  112.3 5.4 %maximum_bitcast_fusion = bf16[8192,4,2,32]{0,1,3,2:T(4,128)(2,1)S(1)} fusion(bf16[8192,1,32,4]{0,3,2,1:T(4,128)(2,1)} %stack_reshape.7, bf16[8192,1,32,4]{0,3,2,1:T(4,128)(2,1)} %stack_reshape.6), kind=kLoop, calls=%fused_computation.14 | loop fusion | flops 2097152 | bytes 8388608 | tf_op jit(solution)/shard_map/transpose | solution.py:158
  117.8 4.3 %copy.65 = bf16[8192,4,2,32]{0,3,2,1:T(8,128)(2,1)} copy(bf16[8192,4,2,32]{0,1,3,2:T(4,128)(2,1)S(1)} %maximum_bitcast_fusion) | data formatting | bytes 8388608 | tf_op jit(solution)/shard_map/transpose | solution.py:158
  122.6 3.4 %all-gather.5.cloned.1.call-done = bf16[64,8192]{1,0:T(8,128)(2,1)} async-done(((bf16[64,2048]{1,0:T(8,128)(2,1)}), bf16[64,8192]{1,0:T(8,128)(2,1)}) %all-gather.5.cloned.1.call-update) | async-done | bytes 1048592 | tf_op jit(solution)/shard_map/all_gather | solution.py:127
  127.6 9.4 %convolution_bitcast_fusion.1 = f32[8,8,8,128]{3,1,2,0:T(8,128)S(1)} fusion(bf16[8192,1024]{1,0:T(8,128)(2,1)} %param.22, bf16[64,8192]{1,0:T(8,128)(2,1)} %all-gather.5.cloned.1.call-done, f32[8192]{0:T(1024)S(1)} %copy-done.8, f32[64]{0:T(128)S(1)} %add_rsqrt_fusion.2), kind=kOutput, calls=%fused_computation.59 | convolution fusion | flops 1075838976 | bytes 18120960 | tf_op jit(solution)/shard_map/dot_general | solution.py:164
  138.6 69.4 %all-gather.7.cloned.1.call-done = bf16[256,8192]{1,0:T(8,128)(2,1)} async-done(((bf16[256,2048]{1,0:T(8,128)(2,1)}), bf16[256,8192]{1,0:T(8,128)(2,1)}) %all-gather.7.cloned.1.call-update) | async-done | bytes 4194320 | tf_op jit(solution)/shard_map/all_gather | solution.py:87
  208.0 3.3 %fusion.2 = f32[256]{0:T(256)S(1)} fusion(bf16[256,8192]{1,0:T(8,128)(2,1)} %all-gather.7.cloned.1.call-done), kind=kLoop, calls=%fused_computation.4 | loop fusion | flops 6291200 | bytes 4195328 | tf_op jit(solution)/shard_map/reduce_sum | solution.py:57
  211.5 4.4 %fusion.39 = bf16[256,256]{1,0:T(8,128)(2,1)S(1)} fusion(bf16[8192,256]{0,1:T(8,128)(2,1)S(1)} %bitcast.115, bf16[256,8192]{1,0:T(8,128)(2,1)} %all-gather.7.cloned.1.call-done, f32[8192]{0:T(1024)S(1)} %copy-done.8, f32[256]{0:T(256)S(1)} %add_rsqrt_fusion), kind=kOutput, calls=%fused_computation.61 | convolution fusion | flops 1082195968 | bytes 8553472 | tf_op jit(solution)/shard_map/dot_general | solution.py:163
  217.0 3.4 %all-to-all-start.1 = ((bf16[4,320,64]{1,2,0:T(8,128)(2,1)}), bf16[4,320,64]{1,2,0:T(8,128)(2,1)S(1)}, u32[]{:S(2)}, u32[]{:S(2)}) async-start(bf16[4,320,64]{1,2,0:T(8,128)(2,1)} %copy.66), calls=%async_computation.2 | async-start | bytes 393216 | tf_op jit(solution)/shard_map/all_to_all | solution.py:180
  220.4 9.5 %convolution_bitcast_fusion = f32[32,8,8,128]{3,1,2,0:T(8,128)S(1)} fusion(bf16[8192,1024]{1,0:T(8,128)(2,1)} %param.22, bf16[256,8192]{1,0:T(8,128)(2,1)} %all-gather.7.cloned.1.call-done, f32[8192]{0:T(1024)S(1)} %copy-done.8, f32[256]{0:T(256)S(1)} %add_rsqrt_fusion), kind=kOutput, calls=%fused_computation.39 | convolution fusion | flops 4303355904 | bytes 22053888 | tf_op jit(solution)/shard_map/dot_general | solution.py:164
  237.4 31.7 %all-gather.11.cloned.1.call-done = bf16[160,4096]{1,0:T(8,128)(2,1)} async-done(((bf16[160,1024]{1,0:T(8,128)(2,1)}), bf16[160,4096]{1,0:T(8,128)(2,1)}) %all-gather.11.cloned.1.call-update) | async-done | bytes 1310736 | tf_op jit(solution)/shard_map/all_gather | solution.py:232
  269.1 10.1 %fusion.141 = f32[160,2048]{1,0:T(8,128)} fusion(bf16[160,4096]{1,0:T(8,128)(2,1)} %all-gather.11.cloned.1.call-done, bf16[4096,2048]{1,0:T(8,128)(2,1)} %param.25), kind=kOutput, calls=%fused_computation.181 | convolution fusion | flops 2684354560 | bytes 19398656 | tf_op jit(solution)/shard_map/dot_general | solution.py:239
  279.3 23.1 %all-gather.9.cloned.1.call-done = bf16[160,4096]{1,0:T(8,128)(2,1)} async-done(((bf16[160,1024]{1,0:T(8,128)(2,1)}), bf16[160,4096]{1,0:T(8,128)(2,1)}) %all-gather.9.cloned.1.call-update) | async-done | bytes 1310736 | tf_op jit(solution)/shard_map/all_gather | solution.py:232
  302.4 7.8 %fusion.140 = f32[160,2048]{1,0:T(8,128)S(1)} fusion(bf16[160,4096]{1,0:T(8,128)(2,1)} %all-gather.9.cloned.1.call-done, bf16[4096,2048]{1,0:T(8,128)(2,1)} %param.25), kind=kOutput, calls=%fused_computation.180 | convolution fusion | flops 2684354560 | bytes 19398656 | tf_op jit(solution)/shard_map/dot_general | solution.py:239
  (94 shorter events, 21.0 us)
Async XLA Ops:
  6.5 1.6 copy-start
  6.5 17.7 %copy-start.10 = (s32[256,1]{0,1:T(1,128)S(1)}, s32[256,1]{0,1:T(1,128)}, u32[]{:S(2)}) copy-start(s32[256,1]{0,1:T(1,128)} %param.14) | copy-start | bytes 3076
  6.5 63.7 %reduce-scatter.2.cloned.1.call-start = ((), (), s32[]{:S(2)}) async-start(), calls=%async_computation.3 | async-start | bytes 2621440 | tf_op jit(solution)/shard_map/reduce_scatter | solution.py:90
  23.5 49.7 %copy-start.9 = (f32[1024]{0:T(1024)S(1)}, f32[1024]{0:T(1024)}, u32[]{:S(2)}) copy-start(f32[1024]{0:T(1024)} %param.19) | copy-start | bytes 12292
  23.6 102.5 %all-gather.5.cloned.1.call-start = ((), (), s32[]{:S(2)}) async-start(), calls=%async_computation.4 | async-start | bytes 1310720 | tf_op jit(solution)/shard_map/all_gather | solution.py:127
  99.6 108.4 %all-gather.7.cloned.1.call-start = ((), (), s32[]{:S(2)}) async-start(), calls=%async_computation.5 | async-start | bytes 5242880 | tf_op jit(solution)/shard_map/all_gather | solution.py:87
  117.7 4.4 %copy-start.11 = (s32[8]{0:T(128)S(1)}, s32[8]{0:T(128)}, u32[]{:S(2)}) copy-start(s32[8]{0:T(128)} %param.15) | copy-start | bytes 100
  117.7 9.9 %copy-start.8 = (f32[8192]{0:T(1024)S(1)}, f32[8192]{0:T(1024)}, u32[]{:S(2)}) copy-start(f32[8192]{0:T(1024)} %param.21) | copy-start | bytes 98308
  127.6 9.6 %copy-start.2 = (bf16[8192,4,2,32]{0,3,2,1:T(8,128)(2,1)S(1)}, bf16[8192,4,2,32]{0,3,2,1:T(8,128)(2,1)}, u32[]{:S(2)}) copy-start(bf16[8192,4,2,32]{0,3,2,1:T(8,128)(2,1)} %copy.65) | copy-start | bytes 12582916
  127.6 9.6 %copy-start.4 = (bf16[64,8192]{1,0:T(8,128)(2,1)S(1)}, bf16[64,8192]{1,0:T(8,128)(2,1)}, u32[]{:S(2)}) copy-start(bf16[64,8192]{1,0:T(8,128)(2,1)} %all-gather.5.cloned.1.call-done) | copy-start | bytes 3145732
  208.0 3.4 %copy-start.3 = (bf16[8192,4,2,32]{0,3,2,1:T(8,128)(2,1)S(1)}, bf16[8192,4,2,32]{0,3,2,1:T(8,128)(2,1)}, u32[]{:S(2)}) copy-start(bf16[8192,4,2,32]{0,3,2,1:T(8,128)(2,1)} %copy.65) | copy-start | bytes 12582916
  217.0 14.3 %all-to-all-start.1 = ((bf16[4,320,64]{1,2,0:T(8,128)(2,1)}), bf16[4,320,64]{1,2,0:T(8,128)(2,1)S(1)}, u32[]{:S(2)}, u32[]{:S(2)}) async-start(bf16[4,320,64]{1,2,0:T(8,128)(2,1)} %copy.66), calls=%async_computation.2 | async-start | bytes 393216 | tf_op jit(solution)/shard_map/all_to_all | solution.py:180
  220.4 48.7 %all-gather.11.cloned.1.call-start = ((), (), s32[]{:S(2)}) async-start(), calls=%async_computation.7 | async-start | bytes 1638400 | tf_op jit(solution)/shard_map/all_gather | solution.py:232
  235.0 67.4 %all-gather.9.cloned.1.call-start = ((), (), s32[]{:S(2)}) async-start(), calls=%async_computation.6 | async-start | bytes 1638400 | tf_op jit(solution)/shard_map/all_gather | solution.py:232
  279.2 30.9 %copy-start.5 = (bf16[8,32,2048]{2,1,0:T(8,128)(2,1)S(1)}, bf16[8,32,2048]{2,1,0:T(8,128)(2,1)}, u32[]{:S(2)}) copy-start(bf16[8,32,2048]{2,1,0:T(8,128)(2,1)} %slice.111) | copy-start | bytes 3145732
  279.3 30.9 %copy-start.7 = (bf16[64,2048]{1,0:T(8,128)(2,1)S(1)}, bf16[64,2048]{1,0:T(8,128)(2,1)}, u32[]{:S(2)}) copy-start(bf16[64,2048]{1,0:T(8,128)(2,1)} %convolution_convert_fusion) | copy-start | bytes 786436
  302.4 7.8 %copy-start.6 = (f32[160,2048]{1,0:T(8,128)S(1)}, f32[160,2048]{1,0:T(8,128)}, u32[]{:S(2)}) copy-start(f32[160,2048]{1,0:T(8,128)} %fusion.141) | copy-start | bytes 3932164
  310.2 2.0 copy-start.1
Sparse Core Ops, SparseCore 0:
  23.7 46.5 reduce-scatter.1
  99.7 26.3 all-gather.4
  127.7 80.2 all-gather.6
  235.1 34.0 all-gather.10
  270.6 31.6 all-gather.8

commit v2 on v1

--- a/solution.py
+++ b/solution.py
@@ -1,8 +1,11 @@
+import functools
 import math
 
 import jax
 import jax.numpy as jnp
 from jax import lax
+from jax.experimental import pallas as pl
+from jax.experimental.pallas import tpu as pltpu
 from jax.sharding import PartitionSpec as P
 
 HQ = 32
@@ -33,22 +36,312 @@
     )
 
 
-def layer_norm(inputs, gain):
-    center = inputs - jnp.mean(inputs, axis=-1, keepdims=True)
+def copy_to(src, dst, send_sem, recv_sem, target):
+    return pltpu.make_async_remote_copy(
+        src_ref=src,
+        dst_ref=dst,
+        send_sem=send_sem,
+        recv_sem=recv_sem,
+        device_id=target,
+        device_id_type=pl.DeviceIdType.MESH,
+    )
+
+
+def front_kernel(
+    n,
+    enc_n,
+    req_n,
+    tokens,
+    enc_up,
+    enc_down,
+    enc_gain,
+    proj_weight,
+    selector,
+    reorder,
+    question_rows,
+    question_full,
+    span_full,
+    partial_out,
+    partial_in,
+    own_sum,
+    pooled,
+    placed,
+    incoming,
+    own_sem,
+    right_send,
+    right_recv,
+    left_send,
+    left_recv,
+    sum_send,
+    sum_recv,
+    pool_send,
+    pool_recv,
+    owner_send,
+    owner_recv,
+    span_send,
+    span_recv,
+):
+    owners = enc_n * req_n
+    me = lax.axis_index("tensor")
+    my_owner = lax.axis_index("enc") * req_n + lax.axis_index("req")
+    share = own_sum.shape[0]
+
+    def tensor_peer(distance):
+        return {"tensor": lax.rem(me + distance, n)}
+
+    def owner_peer(distance):
+        other = lax.rem(my_owner + distance, owners)
+        return other, {"enc": other // req_n, "req": lax.rem(other, req_n)}
+
+    barrier = pltpu.get_barrier_semaphore()
+    for distance in range(1, n):
+        pl.semaphore_signal(
+            barrier,
+            inc=1,
+            device_id=tensor_peer(distance),
+            device_id_type=pl.DeviceIdType.MESH,
+        )
+    for distance in range(1, owners):
+        pl.semaphore_signal(
+            barrier,
+            inc=1,
+            device_id=owner_peer(distance)[1],
+            device_id_type=pl.DeviceIdType.MESH,
+        )
+    pl.semaphore_wait(barrier, n - 1 + owners - 1)
+
+    own_rows = question_rows.at[:, :QUESTION_MAX]
+    own_copy = pltpu.make_async_copy(own_rows, question_full.at[me], own_sem)
+    own_copy.start()
+
+    def rightward(step):
+        block = jnp.maximum(me - step, 0)
+        source = own_rows if step == 0 else question_full.at[block]
+        copy = copy_to(
+            source,
+            question_full.at[block],
+            right_send.at[step],
+            right_recv.at[step],
+            {"tensor": jnp.minimum(me + 1, n - 1)},
+        )
+        return copy, jnp.logical_and(me - step >= 0, me + 1 < n)
+
+    def leftward(step):
+        block = jnp.minimum(me + step, n - 1)
+        source = own_rows if step == 0 else question_full.at[block]
+        copy = copy_to(
+            source,
+            question_full.at[block],
+            left_send.at[step],
+            left_recv.at[step],
+            {"tensor": jnp.maximum(me - 1, 0)},
+        )
+        return copy, jnp.logical_and(me + step < n, me >= 1)
+
+    def send_step(step):
+        for copy, valid in (rightward(step), leftward(step)):
+            pl.when(valid)(copy.start)
+
+    def arrive_step(step):
+        @pl.when(me - 1 - step >= 0)
+        def _():
+            block = jnp.maximum(me - 1 - step, 0)
+            copy_to(
+                own_rows,
+                question_full.at[block],
+                right_send.at[step],
+                right_recv.at[step],
+                {"tensor": jnp.minimum(me + 1, n - 1)},
+            ).wait_recv()
+
+        @pl.when(me + 1 + step < n)
+        def _():
+            block = jnp.minimum(me + 1 + step, n - 1)
+            copy_to(
+                own_rows,
+                question_full.at[block],
+                left_send.at[step],
+                left_recv.at[step],
+                {"tensor": jnp.maximum(me - 1, 0)},
+            ).wait_recv()
+
+    send_step(0)
+
+    def term(place):
+        rows = tokens[pl.ds(pl.multiple_of(place * share, share), share), :]
+        hidden = jnp.dot(rows, enc_up[...], preferred_element_type=jnp.float32)
+        hidden = 0.5 * hidden * (1.0 + lax.erf(hidden * math.sqrt(0.5)))
+        return jnp.dot(
+            hidden.astype(jnp.bfloat16), enc_down[...], preferred_element_type=jnp.float32
+        )
+
+    def sum_copy(slot):
+        return copy_to(
+            partial_out.at[slot],
+            partial_in.at[slot],
+            sum_send.at[slot],
+            sum_recv.at[slot],
+            tensor_peer(slot + 1),
+        )
+
+    @pl.loop(0, n - 1)
+    def _(slot):
+        partial_out[slot] = term(lax.rem(me + slot + 1, n)).astype(jnp.bfloat16)
+        sum_copy(slot).start()
+
+    own_tokens = tokens[pl.ds(pl.multiple_of(me * share, share), share), :]
+    own_sum[...] = term(me) + own_tokens.astype(jnp.float32)
+
+    if n > 2:
+        arrive_step(0)
+        send_step(1)
+
+    for slot in range(n - 1):
+        sum_copy(slot).wait_recv()
+        own_sum[...] += partial_in[slot].astype(jnp.float32)
+    summed = own_sum[...]
+    center = summed - jnp.mean(summed, axis=-1, keepdims=True)
     spread = jnp.mean(center * center, axis=-1, keepdims=True)
-    return center * lax.rsqrt(spread + 1e-05) * gain
-
-
-def ffn_term(token_rows, enc_up, enc_down):
-    enc_hidden = jax.nn.gelu(
-        jnp.dot(token_rows, enc_up, preferred_element_type=jnp.float32), approximate=False
+    encoded = center * lax.rsqrt(spread + 1e-05) * enc_gain[...]
+    pooled[me] = jnp.mean(
+        encoded.reshape(share // SPAN_LEN, SPAN_LEN, encoded.shape[-1]), axis=1
     ).astype(jnp.bfloat16)
-    return jnp.dot(enc_hidden, enc_down, preferred_element_type=jnp.float32)
-
-
-def pool_rows(token_rows, summed, enc_gain):
-    encoded = layer_norm(token_rows.astype(jnp.float32) + summed, enc_gain)
-    return jnp.mean(encoded.reshape(-1, SPAN_LEN, encoded.shape[-1]), axis=1).astype(jnp.bfloat16)
+
+    def pool_copy(slot):
+        return copy_to(
+            pooled.at[me],
+            pooled.at[me],
+            pool_send.at[slot],
+            pool_recv.at[slot],
+            tensor_peer(slot + 1),
+        )
+
+    for slot in range(n - 1):
+        pool_copy(slot).start()
+    for slot in range(n - 1):
+        source = lax.rem(me + n - 1 - slot, n)
+        copy_to(
+            pooled.at[source],
+            pooled.at[source],
+            pool_send.at[slot],
+            pool_recv.at[slot],
+            tensor_peer(slot + 1),
+        ).wait_recv()
+
+    for owner in range(owners):
+        total = jnp.zeros(placed.shape[1:], jnp.float32)
+        for place in range(n):
+            total += jnp.dot(
+                selector[owner, place], pooled[place], preferred_element_type=jnp.float32
+            )
+        placed[owner] = total.astype(jnp.bfloat16)
+    incoming[my_owner] = placed[my_owner]
+
+    def owner_copy(slot):
+        other, target = owner_peer(slot + 1)
+        return copy_to(
+            placed.at[other],
+            incoming.at[my_owner],
+            owner_send.at[slot],
+            owner_recv.at[slot],
+            target,
+        )
+
+    for slot in range(owners - 1):
+        owner_copy(slot).start()
+    for slot in range(owners - 1):
+        source = lax.rem(my_owner + owners - 1 - slot, owners)
+        copy_to(
+            placed.at[source],
+            incoming.at[source],
+            owner_send.at[slot],
+            owner_recv.at[slot],
+            owner_peer(slot + 1)[1],
+        ).wait_recv()
+
+    ordered = jnp.zeros((span_full.shape[1], incoming.shape[2]), jnp.float32)
+    for owner in range(owners):
+        ordered += jnp.dot(
+            reorder[owner], incoming[owner], preferred_element_type=jnp.float32
+        )
+    span_full[me] = jnp.dot(
+        ordered.astype(jnp.bfloat16), proj_weight[...], preferred_element_type=jnp.float32
+    ).astype(jnp.bfloat16)
+
+    def span_copy(slot):
+        return copy_to(
+            span_full.at[me],
+            span_full.at[me],
+            span_send.at[slot],
+            span_recv.at[slot],
+            tensor_peer(slot + 1),
+        )
+
+    for slot in range(n - 1):
+        span_copy(slot).start()
+
+    for step in range(2, n - 1):
+        arrive_step(step - 1)
+        send_step(step)
+    arrive_step(n - 2)
+
+    for slot in range(n - 1):
+        source = lax.rem(me + n - 1 - slot, n)
+        copy_to(
+            span_full.at[source],
+            span_full.at[source],
+            span_send.at[slot],
+            span_recv.at[slot],
+            tensor_peer(slot + 1),
+        ).wait_recv()
+
+    own_copy.wait()
+    for slot in range(n - 1):
+        sum_copy(slot).wait_send()
+        pool_copy(slot).wait_send()
+        span_copy(slot).wait_send()
+        for copy, valid in (rightward(slot), leftward(slot)):
+            pl.when(valid)(copy.wait_send)
+    for slot in range(owners - 1):
+        owner_copy(slot).wait_send()
+
+
+def front(
+    n, enc_n, req_n, tokens, enc_up, enc_down, enc_gain, proj_weight, selector, reorder, rows
+):
+    owners = enc_n * req_n
+    requests, _, columns = rows.shape
+    share = tokens.shape[0] // n
+    width = tokens.shape[1]
+    slots = requests * CAPR
+    vmem = pl.BlockSpec(memory_space=pltpu.VMEM)
+    hbm = pl.BlockSpec(memory_space=pl.ANY)
+    dma = pltpu.SemaphoreType.DMA
+    return pl.pallas_call(
+        functools.partial(front_kernel, n, enc_n, req_n),
+        out_shape=(
+            jax.ShapeDtypeStruct((n, requests, QUESTION_MAX, columns), jnp.bfloat16),
+            jax.ShapeDtypeStruct((n, slots * owners, columns), jnp.bfloat16),
+        ),
+        in_specs=[vmem] * 7 + [hbm],
+        out_specs=(hbm, vmem),
+        scratch_shapes=[
+            pltpu.VMEM((n - 1, share, width), jnp.bfloat16),
+            pltpu.VMEM((n - 1, share, width), jnp.bfloat16),
+            pltpu.VMEM((share, width), jnp.float32),
+            pltpu.VMEM((n, share // SPAN_LEN, width), jnp.bfloat16),
+            pltpu.VMEM((owners, slots, width), jnp.bfloat16),
+            pltpu.VMEM((owners, slots, width), jnp.bfloat16),
+            dma,
+        ]
+        + [dma((n - 1,))] * 8
+        + [dma((owners - 1,))] * 2
+        + [dma((n - 1,))] * 2,
+        compiler_params=pltpu.CompilerParams(
+            collective_id=0, has_side_effects=True, vmem_limit_bytes=40 * 1024 * 1024
+        ),
+        name="front",
+    )(tokens, enc_up, enc_down, enc_gain.reshape(1, -1), proj_weight, selector, reorder, rows)
 
 
 def rms(rows, gain):
@@ -82,23 +375,10 @@
     span_room = CAPR * owner_count
     room = min(SLOT, span_room + QUESTION_MAX)
 
-    questions = question_embed.reshape(requests_here, SLOT, columns)[:, :QUESTION_MAX]
-    questions = questions.reshape(-1, columns)
-    question_full = lax.all_gather(questions, "tensor", axis=1, tiled=True)
-
-    share_rows = span_tokens.shape[0] // tensor_count
-    kept_sums = lax.psum_scatter(
-        ffn_term(span_tokens, enc_up, enc_down).astype(jnp.bfloat16),
-        "tensor",
-        scatter_dimension=0,
-        tiled=True,
-    ).astype(jnp.float32)
-    kept_tokens = lax.dynamic_slice_in_dim(span_tokens, tensor_place * share_rows, share_rows, 0)
-    pooled = lax.all_gather(
-        pool_rows(kept_tokens, kept_sums, enc_gain), "tensor", axis=0, tiled=True
-    )
-
-    spans_here = pooled.shape[0]
+    question_rows = question_embed.reshape(requests_here, SLOT, columns)
+    questions = question_rows[:, :QUESTION_MAX].reshape(-1, columns)
+
+    spans_here = span_tokens.shape[0] // SPAN_LEN
     owners_of = span_request[:, 0]
     all_spans = owners_of.shape[0]
     blocks = owners_of.reshape(owner_count, spans_here)
@@ -111,20 +391,31 @@
     placement = my_spans * CAPR + rank_here
     spot_index = jnp.arange(owner_count * slot_count, dtype=jnp.int32)
     selector = (spot_index[:, None] == placement[None, :]).astype(jnp.bfloat16)
-    placed = jnp.dot(selector, pooled, preferred_element_type=jnp.float32).astype(jnp.bfloat16)
-    incoming = lax.all_to_all(
-        placed.reshape(owner_count, slot_count, -1),
-        ("enc", "req"),
-        split_axis=0,
-        concat_axis=0,
-        tiled=True,
-    )
-    incoming = incoming.reshape(owner_count, requests_here, CAPR, -1)
-    incoming = jnp.swapaxes(incoming, 0, 1).reshape(requests_here * span_room, -1)
-    span_rows = jnp.dot(incoming, proj_weight, preferred_element_type=jnp.float32).astype(
+    selector = selector.reshape(owner_count, slot_count, tensor_count, -1).swapaxes(1, 2)
+    order = jnp.arange(owner_count * slot_count, dtype=jnp.int32)
+    from_row = (
+        order // CAPR % owner_count * slot_count + order // span_room * CAPR + order % CAPR
+    )
+    reorder = (from_row[None, :, None] == order.reshape(owner_count, 1, slot_count)).astype(
         jnp.bfloat16
     )
-    span_full = lax.all_gather(span_rows, "tensor", axis=1, tiled=True)
+    question_full, span_full = front(
+        tensor_count,
+        lax.axis_size("enc"),
+        lax.axis_size("req"),
+        span_tokens,
+        enc_up,
+        enc_down,
+        enc_gain,
+        proj_weight,
+        selector,
+        reorder,
+        question_rows,
+    )
+    span_rows = lax.dynamic_index_in_dim(span_full, tensor_place, 0, keepdims=False)
+    question_full = question_full.reshape(tensor_count, -1, columns)
+    question_full = jnp.swapaxes(question_full, 0, 1).reshape(-1, tensor_count * columns)
+    span_full = jnp.swapaxes(span_full, 0, 1).reshape(-1, tensor_count * columns)
 
     requests_all = requests_here * owner_count
     exact = all_spans == requests_all * span_room
@@ -152,15 +443,27 @@
 
     kv_columns = k_weight.shape[1]
     entries = kv_columns // KVH
-    kv_weight = jnp.stack(
-        [k_weight.reshape(-1, entries, KVH), v_weight.reshape(-1, entries, KVH)], axis=1
-    )
-    kv_weight = jnp.transpose(kv_weight, (0, 3, 1, 2)).reshape(k_weight.shape[0], -1)
+    spot = jnp.arange(2 * kv_columns, dtype=jnp.int32)
+    head_of, kind_of, entry_of = (
+        spot // (2 * entries),
+        spot // entries % 2,
+        spot % entries,
+    )
+    regroup = (
+        spot[:, None] == (kind_of * kv_columns + entry_of * KVH + head_of)[None, :]
+    ).astype(jnp.bfloat16)
     heads_here = q_weight.shape[1] // HD
 
     def project(rows, slots):
         normed = rms(rows, norm_gain)
-        kv = jnp.dot(normed, kv_weight, preferred_element_type=jnp.float32).astype(jnp.bfloat16)
+        kv = jnp.concatenate(
+            [
+                jnp.dot(normed, weight, preferred_element_type=jnp.float32).astype(jnp.bfloat16)
+                for weight in (k_weight, v_weight)
+            ],
+            axis=1,
+        )
+        kv = jnp.dot(kv, regroup, preferred_element_type=jnp.float32).astype(jnp.bfloat16)
         query = jnp.dot(normed, q_weight, preferred_element_type=jnp.float32)
         cosine, sines = rope_tables(slots)
         query = rotate(

time: 319 us -> 351 us (1.10)
  Pallas kernels: 0 us -> 147 us
  waiting for transfers between devices: 173 us -> 50.7 us
  local copies, waits for them, and re-layouts: 23.9 us -> 64.4 us
  blocking collectives: 20.5 us -> 0 us
  matrix products: 65.1 us -> 45.5 us
  other arithmetic: 19.4 us -> 24 us
    pallas_call x0 -> x1, Pallas kernels: none -> 147 us  [front(): pl.pallas_call(functools.partial(front_kernel, n, enc_n, req_n), out_shap...]
    all_gather x2 -> x0, waiting for transfers between devices: 72.8 us -> none  [the longest x1 69.4 us: shards(): question_full = lax.all_gather(questions, 'tensor', axis=1, tiled=True)]
    reduce_scatter x1 -> x0, waiting for transfers between devices: 45 us -> none  [shards(): lax.psum_scatter(ffn_term(span_tokens, enc_up, enc_down).astype(jnp.bfloa...]
    dot_general x5 -> x6, matrix products: 25.2 us -> 3.59 us  [the longest x4 3.19 us: project(): jnp.dot(normed, weight, preferred_element_type=jnp.float32)]
    dot_general x0 -> x1, local copies, waits for them, and re-layouts: none -> 21.3 us  [project(): query = jnp.dot(normed, q_weight, preferred_element_type=jnp.float32)]
    convert_element_type x0 -> x4, local copies, waits for them, and re-layouts: none -> 18.2 us  [the longest x2 9.33 us: rms(): return (wide * lax.rsqrt(jnp.mean(wide * wide, axis=-1, keepdims=True) +...]
    all_gather x1 -> x0, blocking collectives: 13.4 us -> none  [shards(): lax.all_gather(pool_rows(kept_tokens, kept_sums, enc_gain), 'tensor', axi...]
    convert_element_type x1 -> x4, other arithmetic: 0.01 us -> 8.83 us  [the longest x1 4.56 us: rms(): wide = rows.astype(jnp.float32)]
  transfers between devices with their start and end apart: 6 -> 3, of which waited for: 5 -> 2; matrix products, arithmetic and copies ran while one was open for 19% -> 24% of each run, Pallas kernels for 0% -> 0%
where the time goes in v2:
time: 351 us; the launch traced here: 350 us
  Pallas kernels  147 us (42%)
  local copies, waits for them, and re-layouts  64.4 us (18%)
  waiting for transfers between devices  50.7 us (14%)
  matrix products  45.5 us (13%)
  other arithmetic  24 us (7%)
  between operations  13.9 us (4%)
  starting transfers between devices  4.47 us (1%)
    pallas_call x1, Pallas kernels, front(): pl.pallas_call(functools.partial(front_kernel, n, enc_n, req_n), out_shap...  147 us
    all_gather x2, waiting for transfers between devices, attend(): lax.all_gather(context.reshape((high - low) * room, -1), 'tensor', axis=1...  50.7 us
    dot_general x1, local copies, waits for them, and re-layouts, project(): query = jnp.dot(normed, q_weight, preferred_element_type=jnp.float32)  21.3 us
    dot_general x2, matrix products, project(): query = jnp.dot(normed, q_weight, preferred_element_type=jnp.float32)  18.6 us
    dot_general x2, matrix products, shards(): jnp.dot(attend(low, high), o_weight, preferred_element_type=jnp.float32)  17.9 us
    unnamed x41, local copies, waits for them, and re-layouts  12.1 us
    convert_element_type x2, local copies, waits for them, and re-layouts, rms(): return (wide * lax.rsqrt(jnp.mean(wide * wide, axis=-1, keepdims=True) +...  9.33 us
    convert_element_type x2, local copies, waits for them, and re-layouts, rms(): wide = rows.astype(jnp.float32)  8.83 us
  transfers between devices with their start and end apart: 3, of which 2 were waited for; matrix products, arithmetic and copies ran while one was open for 24% of the time, Pallas kernels for 0%

profile of v2, /device:TPU:0, one launch (start us, length us, event | category | flops | bytes accessed | tf_op | source)
XLA Modules:
  0.0 349.9 jit_solution(13271358833862052)
XLA Ops:
  7.1 1.4 reduce.11
  9.1 1.6 copy-done.3
  10.7 1.6 copy-done.5
  12.3 1.6 copy-done.6
  13.9 1.6 copy-done.7
  16.1 147.0 %front.1 = (bf16[4,8,32,2048]{3,2,1,0:T(8,128)(2,1)S(1)}, bf16[4,64,2048]{2,1,0:T(8,128)(2,1)S(1)}) custom-call(bf16[1024,1024]{1,0:T(8,128)(2,1)S(1)} %copy-done.5, bf16[1024,1024]{1,0:T(8,128)(2,1)S(1)} %copy-done.6, bf16[1024,1024]{1,0:T(8,128)(2,1)S(1)} %copy-done.7, f32[1,1024]{1,0:T(1,128)S(1)} %bitcast.126, bf16[1024,2048]{1,0:T(8,128)(2,1)} %proj_weight.1, ...), custom_call_target="tpu_custom_call" | custom-call | tf_op jit(solution)/shard_map/front/pallas_call | solution.py:320
  165.1 4.6 %bitcast_convert_fusion = f32[4,256,2048]{2,1,0:T(8,128)} fusion(bf16[4,8,32,2048]{3,2,1,0:T(8,128)(2,1)S(1)} %get-tuple-element.8), kind=kLoop, calls=%fused_computation.13 | loop fusion | flops 2097152 | bytes 12582912 | tf_op jit(solution)/shard_map/convert_element_type | solution.py:348
  172.6 8.7 %copy.48 = f32[4,256,2048]{1,2,0:T(8,128)} copy(f32[4,256,2048]{2,1,0:T(8,128)} %bitcast_convert_fusion) | data formatting | bytes 16777216 | tf_op jit(solution)/shard_map/convert_element_type | solution.py:348
  181.3 4.1 %fusion.3 = bf16[256,8192]{0,1:T(8,128)(2,1)S(1)} fusion(f32[4,256,2048]{1,2,0:T(8,128)} %copy.48, f32[8192]{0:T(1024)S(1)} %copy-done.14, f32[256]{0:T(256)S(1)} %add_rsqrt_fusion), kind=kLoop, calls=%fused_computation.4 | loop fusion | flops 6291456 | bytes 12616704 | tf_op jit(solution)/shard_map/convert_element_type | solution.py:351
  189.6 4.0 %all-to-all-start = ((bf16[4,320,64]{1,2,0:T(8,128)(2,1)}), bf16[4,320,64]{1,2,0:T(8,128)(2,1)}, u32[]{:S(2)}, u32[]{:S(2)}) async-start(bf16[4,320,64]{1,2,0:T(8,128)(2,1)} %copy.49), calls=%async_computation | async-start | bytes 393216 | tf_op jit(solution)/shard_map/all_to_all | solution.py:483
  194.2 5.7 %fusion.4 = bf16[256,4,2048]{2,0,1:T(8,128)(2,1)} fusion(bf16[4,8,32,2048]{3,2,1,0:T(8,128)(2,1)} %copy-done.2, f32[4,2048]{1,0:T(4,128)S(1)} %mul.395, f32[256]{0:T(256)S(1)} %add_rsqrt_fusion), kind=kLoop, calls=%fused_computation.7 | loop fusion | flops 8388608 | bytes 8422400 | tf_op jit(solution)/shard_map/mul | solution.py:350
  202.5 1.6 reshape.291
  204.1 7.4 %copy.54 = bf16[256,4,2048]{2,1,0:T(4,128)(2,1)} copy(bf16[256,4,2048]{2,0,1:T(8,128)(2,1)} %fusion.4) | data formatting | bytes 8388608 | tf_op jit(solution)/shard_map/mul | solution.py:350
  211.5 7.7 %reshape.293 = bf16[8,32,8192,1]{2,1,0,3:T(8,128)(2,1)} reshape(bf16[256,4,2048]{2,1,0:T(4,128)(2,1)} %copy.54) | data formatting | bytes 8388608 | tf_op jit(solution)/shard_map/convert_element_type | solution.py:351
  219.2 21.3 %copy.76 = bf16[1024,8192]{1,0:T(8,128)(2,1)} copy(bf16[1024,8192]{0,1:T(8,128)(2,1)} %bitcast.129) | data formatting | bytes 33554432 | tf_op jit(solution)/shard_map/dot_general | solution.py:467
  240.5 9.9 %fusion.7 = f32[8,32,8,128]{3,1,2,0:T(8,128)S(1)} fusion(bf16[8,128,8192,1]{2,1,0,3:T(8,128)(2,1)} %bitcast.130, bf16[8,32,8192,1]{2,1,0,3:T(8,128)(2,1)} %reshape.293), kind=kOutput, calls=%fused_computation.11 | convolution fusion | flops 4294967296 | bytes 22020096 | tf_op jit(solution)/shard_map/dot_general | solution.py:467
  250.4 8.7 %fusion.25 = f32[8,8,8,128]{3,1,2,0:T(8,128)S(1)} fusion(bf16[8,128,8192,1]{2,1,0,3:T(8,128)(2,1)} %bitcast.131, bf16[8,8,8192,1]{2,1,0,3:T(8,128)(2,1)S(1)} %copy-done.13), kind=kOutput, calls=%fused_computation.48 | convolution fusion | flops 1073741824 | bytes 18087936 | tf_op jit(solution)/shard_map/dot_general | solution.py:467
  267.3 1.4 fusion.18
  268.7 1.8 fusion.22
  272.6 27.5 %all-gather.3.cloned.1.call-done = bf16[160,4096]{1,0:T(8,128)(2,1)} async-done(((bf16[160,1024]{1,0:T(8,128)(2,1)}), bf16[160,4096]{1,0:T(8,128)(2,1)}) %all-gather.3.cloned.1.call-update) | async-done | bytes 1310736 | tf_op jit(solution)/shard_map/all_gather | solution.py:535
  300.0 10.1 %fusion.109 = f32[160,2048]{1,0:T(8,128)} fusion(bf16[160,4096]{1,0:T(8,128)(2,1)} %all-gather.3.cloned.1.call-done, bf16[4096,2048]{1,0:T(8,128)(2,1)} %param.25), kind=kOutput, calls=%fused_computation.173 | convolution fusion | flops 2684354560 | bytes 19398656 | tf_op jit(solution)/shard_map/dot_general | solution.py:542
  310.2 23.2 %all-gather.5.cloned.1.call-done = bf16[160,4096]{1,0:T(8,128)(2,1)} async-done(((bf16[160,1024]{1,0:T(8,128)(2,1)}), bf16[160,4096]{1,0:T(8,128)(2,1)}) %all-gather.5.cloned.1.call-update) | async-done | bytes 1310736 | tf_op jit(solution)/shard_map/all_gather | solution.py:535
  333.3 7.8 %fusion.110 = f32[160,2048]{1,0:T(8,128)S(1)} fusion(bf16[160,4096]{1,0:T(8,128)(2,1)} %all-gather.5.cloned.1.call-done, bf16[4096,2048]{1,0:T(8,128)(2,1)} %param.25), kind=kOutput, calls=%fused_computation.174 | convolution fusion | flops 2684354560 | bytes 19398656 | tf_op jit(solution)/shard_map/dot_general | solution.py:542
  341.5 1.6 fusion.12
  (100 shorter events, 24.2 us)
Async XLA Ops:
  6.5 163.3 %copy-start = (bf16[8192,128]{1,0:T(8,128)(2,1)S(1)}, bf16[8192,128]{1,0:T(8,128)(2,1)}, u32[]{:S(2)}) copy-start(bf16[8192,128]{1,0:T(8,128)(2,1)} %param.24) | copy-start | bytes 6291460
  9.1 1.6 copy-start.3
  10.7 1.6 copy-start.5
  12.3 1.6 copy-start.6
  13.9 1.6 copy-start.7
  15.4 0.7 copy-start.8
  163.2 1.9 copy-start.2
  169.7 0.8 copy-start.14
  170.5 1.6 copy-start.11
  185.4 1.6 copy-start.12
  189.6 71.7 %all-to-all-start = ((bf16[4,320,64]{1,2,0:T(8,128)(2,1)}), bf16[4,320,64]{1,2,0:T(8,128)(2,1)}, u32[]{:S(2)}, u32[]{:S(2)}) async-start(bf16[4,320,64]{1,2,0:T(8,128)(2,1)} %copy.49), calls=%async_computation | async-start | bytes 393216 | tf_op jit(solution)/shard_map/all_to_all | solution.py:483
  193.6 106.5 %all-gather.3.cloned.1.call-start = ((), (), s32[]{:S(2)}) async-start(), calls=%async_computation.1 | async-start | bytes 1638400 | tf_op jit(solution)/shard_map/all_gather | solution.py:535
  194.2 5.7 %copy-start.17 = (s32[8]{0:T(128)S(1)}, s32[8]{0:T(128)}, u32[]{:S(2)}) copy-start(s32[8]{0:T(128)} %param.15) | copy-start | bytes 100
  240.5 9.9 %copy-start.13 = (bf16[8,8,8192,1]{2,1,0,3:T(8,128)(2,1)S(1)}, bf16[8,8,8192,1]{2,1,0,3:T(8,128)(2,1)}, u32[]{:S(2)}) copy-start(bf16[8,8,8192,1]{2,1,0,3:T(8,128)(2,1)} %reshape.291) | copy-start | bytes 3145732
  259.2 1.4 copy-start.15
  259.2 1.4 copy-start.16
  266.4 66.9 %all-gather.5.cloned.1.call-start = ((), (), s32[]{:S(2)}) async-start(), calls=%async_computation.2 | async-start | bytes 1638400 | tf_op jit(solution)/shard_map/all_gather | solution.py:535
  268.7 2.7 copy-start.4
  310.2 31.0 %copy-start.10 = (bf16[8,32,2048]{2,1,0:T(8,128)(2,1)S(1)}, bf16[8,32,2048]{2,1,0:T(8,128)(2,1)}, u32[]{:S(2)}) copy-start(bf16[8,32,2048]{2,1,0:T(8,128)(2,1)} %slice.111) | copy-start | bytes 3145732
  333.3 7.8 %copy-start.9 = (f32[160,2048]{1,0:T(8,128)S(1)}, f32[160,2048]{1,0:T(8,128)}, u32[]{:S(2)}) copy-start(f32[160,2048]{1,0:T(8,128)} %fusion.109) | copy-start | bytes 3932164
  341.2 1.9 copy-start.1
Sparse Core Ops, SparseCore 0:
  266.5 33.4 all-gather.2
  301.6 31.6 all-gather.4

commit v3 on v2

--- a/solution.py
+++ b/solution.py
@@ -344,11 +344,261 @@
     )(tokens, enc_up, enc_down, enc_gain.reshape(1, -1), proj_weight, selector, reorder, rows)
 
 
-def rms(rows, gain):
-    wide = rows.astype(jnp.float32)
-    return (
-        wide * lax.rsqrt(jnp.mean(wide * wide, axis=-1, keepdims=True) + 1e-05) * gain
-    ).astype(jnp.bfloat16)
+def project_kernel(
+    heads,
+    gain,
+    question_rows,
+    span_rows,
+    q_weight,
+    k_weight,
+    v_weight,
+    regroup,
+    cosine,
+    sines,
+    queries,
+    kv,
+    squares,
+    q_sum,
+    kv_sum,
+):
+    step = pl.program_id(0)
+    kv_columns = k_weight.shape[1]
+
+    @pl.when(step == 0)
+    def _():
+        squares[...] = jnp.zeros_like(squares)
+        q_sum[...] = jnp.zeros_like(q_sum)
+        kv_sum[...] = jnp.zeros_like(kv_sum)
+
+    low = 0
+    for part in (question_rows, span_rows):
+        size = part.shape[1]
+        rows = part[0].astype(jnp.float32)
+        squares[low : low + size, :] += jnp.broadcast_to(
+            jnp.sum(rows * rows, axis=-1, keepdims=True), (size, squares.shape[1])
+        )
+        scaled = (rows * gain[0]).astype(jnp.bfloat16)
+        q_sum[low : low + size, :] += jnp.dot(
+            scaled, q_weight[...], preferred_element_type=jnp.float32
+        )
+        kv_sum[0, low : low + size, :] += jnp.dot(
+            scaled, k_weight[...], preferred_element_type=jnp.float32
+        )
+        kv_sum[1, low : low + size, :] += jnp.dot(
+            scaled, v_weight[...], preferred_element_type=jnp.float32
+        )
+        low += size
+
+    @pl.when(step == pl.num_programs(0) - 1)
+    def _():
+        features = gain.shape[2] * pl.num_programs(0)
+        scale = lax.rsqrt(squares[...] / features + 1e-05)
+        for head in range(heads):
+            part = q_sum[:, head * HD : (head + 1) * HD] * scale
+            turned = part * cosine[...] + pltpu.roll(part, HD // 2, 1) * sines[...]
+            queries[:, head * HD : (head + 1) * HD] = turned.astype(jnp.bfloat16)
+        narrow = scale[:, :kv_columns]
+        kv[...] = (
+            jnp.dot(
+                (kv_sum[0] * narrow).astype(jnp.bfloat16),
+                regroup[0],
+                preferred_element_type=jnp.float32,
+            )
+            + jnp.dot(
+                (kv_sum[1] * narrow).astype(jnp.bfloat16),
+                regroup[1],
+                preferred_element_type=jnp.float32,
+            )
+        ).astype(jnp.bfloat16)
+
+
+def project(question_full, span_full, gain, q_weight, k_weight, v_weight, regroup, cosine, sines):
+    n, question_count, columns = question_full.shape
+    span_count = span_full.shape[1]
+    count = question_count + span_count
+    q_columns, kv_columns = q_weight.shape[1], k_weight.shape[1]
+    whole = pl.BlockSpec(memory_space=pltpu.VMEM)
+    return pl.pallas_call(
+        functools.partial(project_kernel, q_columns // HD),
+        grid=(n,),
+        out_shape=(
+            jax.ShapeDtypeStruct((count, q_columns), jnp.bfloat16),
+            jax.ShapeDtypeStruct((count, 2 * kv_columns), jnp.bfloat16),
+        ),
+        in_specs=[
+            pl.BlockSpec((1, 1, columns), lambda t: (t, 0, 0)),
+            pl.BlockSpec((1, question_count, columns), lambda t: (t, 0, 0)),
+            pl.BlockSpec((1, span_count, columns), lambda t: (t, 0, 0)),
+            pl.BlockSpec((columns, q_columns), lambda t: (t, 0)),
+            pl.BlockSpec((columns, kv_columns), lambda t: (t, 0)),
+            pl.BlockSpec((columns, kv_columns), lambda t: (t, 0)),
+            whole,
+            whole,
+            whole,
+        ],
+        out_specs=(whole, whole),
+        scratch_shapes=[
+            pltpu.VMEM((count, HD), jnp.float32),
+            pltpu.VMEM((count, q_columns), jnp.float32),
+            pltpu.VMEM((2, count, kv_columns), jnp.float32),
+        ],
+        compiler_params=pltpu.CompilerParams(vmem_limit_bytes=48 * 1024 * 1024),
+        name="project",
+    )(
+        gain.reshape(n, 1, columns),
+        question_full,
+        span_full,
+        q_weight,
+        k_weight,
+        v_weight,
+        regroup,
+        cosine,
+        sines,
+    )
+
+
+def back_kernel(
+    n,
+    room,
+    context,
+    o_weight,
+    local_rows,
+    live_rows,
+    out,
+    blocks,
+    weights,
+    total,
+    weight_sem,
+    right_send,
+    right_recv,
+    left_send,
+    left_recv,
+):
+    me = lax.axis_index("tensor")
+    depth = context.shape[1]
+    weight_copy = pltpu.make_async_copy(o_weight, weights, weight_sem)
+    weight_copy.start()
+    blocks[me] = context[...]
+
+    barrier = pltpu.get_barrier_semaphore()
+    for distance in range(1, n):
+        pl.semaphore_signal(
+            barrier,
+            inc=1,
+            device_id={"tensor": lax.rem(me + distance, n)},
+            device_id_type=pl.DeviceIdType.MESH,
+        )
+    pl.semaphore_wait(barrier, n - 1)
+
+    def rightward(block, step):
+        return copy_to(
+            blocks.at[block],
+            blocks.at[block],
+            right_send.at[step],
+            right_recv.at[step],
+            {"tensor": jnp.minimum(me + 1, n - 1)},
+        )
+
+    def leftward(block, step):
+        return copy_to(
+            blocks.at[block],
+            blocks.at[block],
+            left_send.at[step],
+            left_recv.at[step],
+            {"tensor": jnp.maximum(me - 1, 0)},
+        )
+
+    def send_step(step):
+        @pl.when(jnp.logical_and(me - step >= 0, me + 1 < n))
+        def _():
+            rightward(jnp.maximum(me - step, 0), step).start()
+
+        @pl.when(jnp.logical_and(me + step < n, me >= 1))
+        def _():
+            leftward(jnp.minimum(me + step, n - 1), step).start()
+
+    tile = min(512, out.shape[2])
+
+    def multiply(block):
+        rows = pl.ds(pl.multiple_of(block * depth, depth), depth)
+
+        @pl.loop(0, out.shape[2] // tile)
+        def _(column):
+            at = pl.ds(pl.multiple_of(column * tile, tile), tile)
+            total[:, at] += jnp.dot(
+                blocks[block], weights[rows, at], preferred_element_type=jnp.float32
+            )
+
+    send_step(0)
+    total[...] = local_rows[...].astype(jnp.float32)
+    weight_copy.wait()
+    multiply(me)
+
+    @pl.loop(0, n - 1)
+    def _(step):
+        left_block = jnp.maximum(me - 1 - step, 0)
+        right_block = jnp.minimum(me + 1 + step, n - 1)
+
+        @pl.when(me - 1 - step >= 0)
+        def _():
+            rightward(left_block, step).wait_recv()
+
+        @pl.when(me + 1 + step < n)
+        def _():
+            leftward(right_block, step).wait_recv()
+
+        @pl.when(step + 1 < n - 1)
+        def _():
+            send_step(step + 1)
+
+        @pl.when(me - 1 - step >= 0)
+        def _():
+            multiply(left_block)
+
+        @pl.when(me + 1 + step < n)
+        def _():
+            multiply(right_block)
+
+    requests = out.shape[0]
+    for request in range(requests):
+        rows = slice(request * room, (request + 1) * room)
+        kept = total[rows, :] * live_rows[rows, :1]
+        rest = jnp.zeros((out.shape[1] - room, out.shape[2]), jnp.float32)
+        out[request] = jnp.concatenate([kept, rest], axis=0).astype(jnp.bfloat16)
+
+    @pl.loop(0, n - 1)
+    def _(step):
+        @pl.when(jnp.logical_and(me - step >= 0, me + 1 < n))
+        def _():
+            rightward(jnp.maximum(me - step, 0), step).wait_send()
+
+        @pl.when(jnp.logical_and(me + step < n, me >= 1))
+        def _():
+            leftward(jnp.minimum(me + step, n - 1), step).wait_send()
+
+
+def back(n, room, context, o_weight, local_rows, live_rows):
+    count, depth = context.shape
+    columns = o_weight.shape[1]
+    vmem = pl.BlockSpec(memory_space=pltpu.VMEM)
+    dma = pltpu.SemaphoreType.DMA
+    return pl.pallas_call(
+        functools.partial(back_kernel, n, room),
+        out_shape=jax.ShapeDtypeStruct((count // room, SLOT, columns), jnp.bfloat16),
+        in_specs=[vmem, pl.BlockSpec(memory_space=pl.ANY), vmem, vmem],
+        out_specs=vmem,
+        scratch_shapes=[
+            pltpu.VMEM((n, count, depth), jnp.bfloat16),
+            pltpu.VMEM(o_weight.shape, jnp.bfloat16),
+            pltpu.VMEM((count, columns), jnp.float32),
+            dma,
+        ]
+        + [dma((n - 1,))] * 4,
+        compiler_params=pltpu.CompilerParams(
+            collective_id=1, has_side_effects=True, vmem_limit_bytes=48 * 1024 * 1024
+        ),
+        name="back",
+    )(context, o_weight, local_rows, live_rows)
 
 
 def shards(
@@ -414,8 +664,6 @@
     )
     span_rows = lax.dynamic_index_in_dim(span_full, tensor_place, 0, keepdims=False)
     question_full = question_full.reshape(tensor_count, -1, columns)
-    question_full = jnp.swapaxes(question_full, 0, 1).reshape(-1, tensor_count * columns)
-    span_full = jnp.swapaxes(span_full, 0, 1).reshape(-1, tensor_count * columns)
 
     requests_all = requests_here * owner_count
     exact = all_spans == requests_all * span_room
@@ -451,32 +699,41 @@
     )
     regroup = (
         spot[:, None] == (kind_of * kv_columns + entry_of * KVH + head_of)[None, :]
-    ).astype(jnp.bfloat16)
+    ).astype(jnp.bfloat16).reshape(2, kv_columns, 2 * kv_columns)
     heads_here = q_weight.shape[1] // HD
 
-    def project(rows, slots):
-        normed = rms(rows, norm_gain)
-        kv = jnp.concatenate(
+    question_slots = requests_here * QUESTION_MAX
+    cosine, sines = rope_tables(
+        jnp.concatenate(
             [
-                jnp.dot(normed, weight, preferred_element_type=jnp.float32).astype(jnp.bfloat16)
-                for weight in (k_weight, v_weight)
+                slot_positions[:, span_room:].reshape(-1),
+                slot_positions[:, :span_room].reshape(-1),
+            ]
+        )
+    )
+    queries, kv = project(
+        question_full,
+        span_full,
+        norm_gain,
+        q_weight,
+        k_weight,
+        v_weight,
+        regroup,
+        jnp.concatenate([cosine, cosine], axis=1),
+        jnp.concatenate([-sines, sines], axis=1),
+    )
+
+    def by_request(rows):
+        return jnp.concatenate(
+            [
+                rows[question_slots:].reshape(requests_here, span_room, -1),
+                rows[:question_slots].reshape(requests_here, QUESTION_MAX, -1),
             ],
             axis=1,
         )
-        kv = jnp.dot(kv, regroup, preferred_element_type=jnp.float32).astype(jnp.bfloat16)
-        query = jnp.dot(normed, q_weight, preferred_element_type=jnp.float32)
-        cosine, sines = rope_tables(slots)
-        query = rotate(
-            query.reshape(requests_here, -1, heads_here, HD),
-            cosine[:, :, None, :],
-            sines[:, :, None, :],
-        ).astype(jnp.bfloat16)
-        return query, kv.reshape(requests_here, -1, 2 * kv_columns)
-
-    question_queries, question_kv = project(question_full, slot_positions[:, span_room:])
-    span_queries, span_kv = project(span_full, slot_positions[:, :span_room])
-    queries = jnp.concatenate([span_queries, question_queries], axis=1)
-    kv = jnp.concatenate([span_kv, question_kv], axis=1)
+
+    queries = by_request(queries).reshape(requests_here, -1, heads_here, HD)
+    kv = by_request(kv)
     slots = kv.shape[1]
     if tensor_count == KVH:
         kv = kv.reshape(requests_here * slots, KVH, 2 * entries)
@@ -511,44 +768,33 @@
         ).astype(jnp.bfloat16)
     live_rows = jnp.arange(room, dtype=jnp.int32)[None, :] < (counts + question_length)[:, None]
 
-    def attend(low, high):
-        scores = jnp.einsum(
-            "rphd,rqd->rhpq",
-            queries[low:high],
-            keys[low:high],
-            preferred_element_type=jnp.float32,
-        ) * HD ** (-0.5)
-        spots = slot_positions[low:high]
-        allowed = jnp.logical_and(
-            spots[:, :, None] >= spots[:, None, :], live[low:high][:, None, :]
-        )
-        scores = jnp.where(allowed[:, None], scores, -1e30)
-        probs = jax.nn.softmax(scores, axis=-1).astype(jnp.bfloat16)
+    scores = jnp.einsum(
+        "rphd,rqd->rhpq", queries, keys, preferred_element_type=jnp.float32
+    ) * HD ** (-0.5)
+    allowed = jnp.logical_and(
+        slot_positions[:, :, None] >= slot_positions[:, None, :], live[:, None, :]
+    )
+    scores = jnp.where(allowed[:, None], scores, -1e30)
+    probs = jax.nn.softmax(scores, axis=-1).astype(jnp.bfloat16)
+    context = jnp.einsum(
+        "rhpq,rqd->rphd", probs, values, preferred_element_type=jnp.float32
+    ).astype(jnp.bfloat16)
+    context = context.reshape(requests_here, slots, heads_here * HD)
+    if not exact:
         context = jnp.einsum(
-            "rhpq,rqd->rphd", probs, values[low:high], preferred_element_type=jnp.float32
+            "rps,rsc->rpc", order, context, preferred_element_type=jnp.float32
         ).astype(jnp.bfloat16)
-        context = context.reshape(high - low, slots, heads_here * HD)
-        if not exact:
-            context = jnp.einsum(
-                "rps,rsc->rpc", order[low:high], context, preferred_element_type=jnp.float32
-            ).astype(jnp.bfloat16)
-        return lax.all_gather(
-            context.reshape((high - low) * room, -1), "tensor", axis=1, tiled=True
-        )
-
-    half = requests_here // 2
-    outs = []
-    for low, high in ((0, half), (half, requests_here)):
-        mixed = jnp.dot(attend(low, high), o_weight, preferred_element_type=jnp.float32)
-        mixed = mixed.reshape(high - low, room, columns)
-        summed = local_rows[low:high].astype(jnp.float32) + mixed
-        outs.append(
-            jnp.where(live_rows[low:high][:, :, None], summed, jnp.zeros_like(summed)).astype(
-                jnp.bfloat16
-            )
-        )
-    out = jnp.concatenate(outs, axis=0)
-    return jnp.pad(out, ((0, 0), (0, SLOT - room), (0, 0))).reshape(-1, columns)
+    out = back(
+        tensor_count,
+        room,
+        context.reshape(requests_here * room, -1),
+        o_weight,
+        local_rows.reshape(requests_here * room, columns),
+        jnp.broadcast_to(
+            live_rows.astype(jnp.float32).reshape(-1, 1), (requests_here * room, 128)
+        ),
+    )
+    return out.reshape(-1, columns)
 
 
 def solution(mesh):

time: 351 us -> 243 us (0.69)
  Pallas kernels: 147 us -> 209 us
  waiting for transfers between devices: 50.7 us -> 1.98 us
  local copies, waits for them, and re-layouts: 64.4 us -> 19.7 us
  matrix products: 45.5 us -> 3.83 us
  other arithmetic: 24 us -> 3.94 us
  between operations: 13.9 us -> 0.32 us
    pallas_call x0 -> x2, Pallas kernels: none -> 61.7 us  [the longest x1 47.6 us: back(): pl.pallas_call(functools.partial(back_kernel, n, room), out_shape=jax.Sha...]
    all_gather x2 -> x0, waiting for transfers between devices: 50.7 us -> none  [attend(): lax.all_gather(context.reshape((high - low) * room, -1), 'tensor', axis=1...]
    dot_general x14 -> x1, matrix products: 44.3 us -> 1.7 us  [shards(): jnp.einsum('rhpq,rqd->rphd', probs, values, preferred_element_type=jnp.fl...]
    dot_general x1 -> x0, local copies, waits for them, and re-layouts: 21.3 us -> none  [project(): query = jnp.dot(normed, q_weight, preferred_element_type=jnp.float32)]
    convert_element_type x6 -> x2, local copies, waits for them, and re-layouts: 18.2 us -> 0.17 us  [the longest x1 0.09 us: shards(): context = jnp.einsum('rhpq,rqd->rphd', probs, values, preferred_element_t...]
    convert_element_type x3 -> x2, other arithmetic: 9.03 us -> 0.18 us  [the longest x1 0.1 us: shards(): regroup = (spot[:, None] == (kind_of * kv_columns + entry_of * KVH + head...]
    mul x3 -> x0, local copies, waits for them, and re-layouts: 8.22 us -> none  [rms(): wide * lax.rsqrt(jnp.mean(wide * wide, axis=-1, keepdims=True) + 1e-05)]
    mul x2 -> x0, other arithmetic: 6.06 us -> none  [rms(): wide * lax.rsqrt(jnp.mean(wide * wide, axis=-1, keepdims=True) + 1e-05)]
  transfers between devices with their start and end apart: 3 -> 1, of which waited for: 2 -> 1; matrix products, arithmetic and copies ran while one was open for 24% -> 2% of each run, Pallas kernels for 0% -> 0%
where the time goes in v3:
time: 243 us; the launch traced here: 242 us
  Pallas kernels  209 us (86%)
  local copies, waits for them, and re-layouts  19.7 us (8%)
  other arithmetic  3.94 us (2%)
  matrix products  3.83 us (2%)
  starting transfers between devices  3.54 us (1%)
    pallas_call x1, Pallas kernels, front(): pl.pallas_call(functools.partial(front_kernel, n, enc_n, req_n), out_shap...  147 us
    pallas_call x1, Pallas kernels, back(): pl.pallas_call(functools.partial(back_kernel, n, room), out_shape=jax.Sha...  47.6 us
    unnamed x33, local copies, waits for them, and re-layouts  14.2 us
    pallas_call x1, Pallas kernels, project(): pl.pallas_call(functools.partial(project_kernel, q_columns // HD), grid=(...  14.1 us
  transfers between devices with their start and end apart: 1, of which 1 were waited for; matrix products, arithmetic and copies ran while one was open for 2% of the time, Pallas kernels for 0%

profile of v3, /device:TPU:0, one launch (start us, length us, event | category | flops | bytes accessed | tf_op | source)
XLA Modules:
  0.0 242.2 jit_solution(6302651748775212741)
XLA Ops:
  0.1 0.5 broadcast.320
  0.6 1.3 reduce.7
  2.8 0.7 fusion.21
  3.7 1.6 copy-done
  5.3 1.6 copy-done.4
  6.9 1.6 copy-done.5
  8.5 1.6 copy-done.6
  10.1 147.2 %front.1 = (bf16[4,8,32,2048]{3,2,1,0:T(8,128)(2,1)S(1)}, bf16[4,64,2048]{2,1,0:T(8,128)(2,1)S(1)}) custom-call(bf16[1024,1024]{1,0:T(8,128)(2,1)S(1)} %copy-done.4, bf16[1024,1024]{1,0:T(8,128)(2,1)S(1)} %copy-done.5, bf16[1024,1024]{1,0:T(8,128)(2,1)S(1)} %copy-done.6, f32[1,1024]{1,0:T(1,128)S(1)} %bitcast.70, bf16[1024,2048]{1,0:T(8,128)(2,1)} %proj_weight.1, ...), custom_call_target="tpu_custom_call" | custom-call | tf_op jit(solution)/shard_map/front/pallas_call | solution.py:320
  157.3 1.9 copy-done.2
  159.2 14.1 %project.1 = (bf16[320,1024]{1,0:T(8,128)(2,1)S(1)}, bf16[320,256]{1,0:T(8,128)(2,1)S(1)}) custom-call(f32[4,1,2048]{2,1,0:T(1,128)S(1)} %bitcast.69, bf16[4,256,2048]{2,1,0:T(8,128)(2,1)} %bitcast.67, bf16[4,64,2048]{2,1,0:T(8,128)(2,1)S(1)} %get-tuple-element.10.span_rows, bf16[8192,1024]{1,0:T(8,128)(2,1)} %q_weight.1, bf16[8192,128]{1,0:T(8,128)(2,1)S(1)} %copy-done.3, ...), custom_call_target="tpu_custom_call" | custom-call | tf_op jit(solution)/shard_map/project/pallas_call | solution.py:421
  173.4 0.8 copy-done.7
  174.2 0.7 pad_maximum_fusion.3
  174.9 1.3 reshape.253
  176.2 0.9 copy.29
  177.1 3.5 %all-to-all-start = ((bf16[4,320,64]{1,2,0:T(8,128)(2,1)}), bf16[4,320,64]{1,2,0:T(8,128)(2,1)S(1)}, u32[]{:S(2)}, u32[]{:S(2)}) async-start(bf16[4,320,64]{1,2,0:T(8,128)(2,1)} %copy.29), calls=%async_computation | async-start | bytes 393216 | tf_op jit(solution)/shard_map/all_to_all | solution.py:740
  180.6 1.9 slice_bitcast_fusion
  182.5 0.9 slice_bitcast_fusion.1
  183.4 1.0 slice.52
  184.9 0.5 copy-done.12
  186.0 2.0 all-to-all-done
  189.1 2.1 fusion.49
  191.2 1.7 fusion.5
  193.3 47.6 %back.1 = bf16[8,64,2048]{2,1,0:T(8,128)(2,1)S(1)} custom-call(bf16[320,1024]{1,0:T(8,128)(2,1)S(1)} %bitcast.68, bf16[4096,2048]{1,0:T(8,128)(2,1)} %o_weight.1, bf16[320,2048]{1,0:T(8,128)(2,1)S(1)} %bitcast.64, f32[320,128]{1,0:T(8,128)S(1)} %broadcast_in_dim.21.live_rows), custom_call_target="tpu_custom_call" | custom-call | tf_op jit(solution)/shard_map/back/pallas_call | solution.py:585
  240.8 1.3 copy.51
  (63 shorter events, 3.6 us)
Async XLA Ops:
  0.0 3.7 %copy-start.9 = (f32[1024]{0:T(1024)S(1)}, f32[1024]{0:T(1024)}, u32[]{:S(2)}) copy-start(f32[1024]{0:T(1024)} %param.19) | copy-start | bytes 12292
  3.7 1.6 copy-start
  5.3 1.6 copy-start.4
  6.9 1.6 copy-start.5
  8.5 1.6 copy-start.6
  10.1 149.2 %copy-start.3 = (bf16[8192,128]{1,0:T(8,128)(2,1)S(1)}, bf16[8192,128]{1,0:T(8,128)(2,1)}, u32[]{:S(2)}) copy-start(bf16[8192,128]{1,0:T(8,128)(2,1)} %k_weight.1) | copy-start | bytes 6291460
  10.1 149.2 %copy-start.8 = (f32[8192]{0:T(1024)S(1)}, f32[8192]{0:T(1024)}, u32[]{:S(2)}) copy-start(f32[8192]{0:T(1024)} %param.21) | copy-start | bytes 98308
  157.3 1.9 copy-start.2
  173.4 0.8 copy-start.7
  174.9 8.5 %copy-start.1 = (bf16[512,2048]{1,0:T(8,128)(2,1)S(1)}, bf16[512,2048]{1,0:T(8,128)(2,1)}, u32[]{:S(2)}) copy-start(bf16[512,2048]{1,0:T(8,128)(2,1)} %param.16) | copy-start | bytes 6291460
  177.1 11.0 %all-to-all-start = ((bf16[4,320,64]{1,2,0:T(8,128)(2,1)}), bf16[4,320,64]{1,2,0:T(8,128)(2,1)S(1)}, u32[]{:S(2)}, u32[]{:S(2)}) async-start(bf16[4,320,64]{1,2,0:T(8,128)(2,1)} %copy.29), calls=%async_computation | async-start | bytes 393216 | tf_op jit(solution)/shard_map/all_to_all | solution.py:740
  183.4 1.2 copy-start.11
  184.6 0.7 copy-start.12
  184.7 1.2 copy-start.10

commit v4 on v3

--- a/solution.py
+++ b/solution.py
@@ -51,16 +51,21 @@
     n,
     enc_n,
     req_n,
-    tokens,
-    enc_up,
-    enc_down,
+    tokens_hbm,
+    up_hbm,
+    down_hbm,
+    proj_hbm,
     enc_gain,
-    proj_weight,
     selector,
     reorder,
     question_rows,
     question_full,
     span_full,
+    tokens,
+    enc_up,
+    enc_down,
+    proj_weight,
+    load_sem,
     partial_out,
     partial_in,
     own_sum,
@@ -85,6 +90,14 @@
     me = lax.axis_index("tensor")
     my_owner = lax.axis_index("enc") * req_n + lax.axis_index("req")
     share = own_sum.shape[0]
+    loads = [
+        pltpu.make_async_copy(source, kept, load_sem.at[place])
+        for place, (source, kept) in enumerate(
+            ((tokens_hbm, tokens), (up_hbm, enc_up), (down_hbm, enc_down), (proj_hbm, proj_weight))
+        )
+    ]
+    for load in loads:
+        load.start()
 
     def tensor_peer(distance):
         return {"tensor": lax.rem(me + distance, n)}
@@ -183,6 +196,9 @@
             sum_recv.at[slot],
             tensor_peer(slot + 1),
         )
+
+    for load in loads[:3]:
+        load.wait()
 
     @pl.loop(0, n - 1)
     def _(slot):
@@ -218,6 +234,9 @@
 
     for slot in range(n - 1):
         pool_copy(slot).start()
+    if n > 3:
+        arrive_step(1)
+        send_step(2)
     for slot in range(n - 1):
         source = lax.rem(me + n - 1 - slot, n)
         copy_to(
@@ -264,6 +283,7 @@
         ordered += jnp.dot(
             reorder[owner], incoming[owner], preferred_element_type=jnp.float32
         )
+    loads[3].wait()
     span_full[me] = jnp.dot(
         ordered.astype(jnp.bfloat16), proj_weight[...], preferred_element_type=jnp.float32
     ).astype(jnp.bfloat16)
@@ -280,7 +300,7 @@
     for slot in range(n - 1):
         span_copy(slot).start()
 
-    for step in range(2, n - 1):
+    for step in range(3, n - 1):
         arrive_step(step - 1)
         send_step(step)
     arrive_step(n - 2)
@@ -323,9 +343,14 @@
             jax.ShapeDtypeStruct((n, requests, QUESTION_MAX, columns), jnp.bfloat16),
             jax.ShapeDtypeStruct((n, slots * owners, columns), jnp.bfloat16),
         ),
-        in_specs=[vmem] * 7 + [hbm],
+        in_specs=[hbm] * 4 + [vmem] * 3 + [hbm],
         out_specs=(hbm, vmem),
         scratch_shapes=[
+            pltpu.VMEM(tokens.shape, jnp.bfloat16),
+            pltpu.VMEM(enc_up.shape, jnp.bfloat16),
+            pltpu.VMEM(enc_down.shape, jnp.bfloat16),
+            pltpu.VMEM(proj_weight.shape, jnp.bfloat16),
+            dma((4,)),
             pltpu.VMEM((n - 1, share, width), jnp.bfloat16),
             pltpu.VMEM((n - 1, share, width), jnp.bfloat16),
             pltpu.VMEM((share, width), jnp.float32),
@@ -338,10 +363,10 @@
         + [dma((owners - 1,))] * 2
         + [dma((n - 1,))] * 2,
         compiler_params=pltpu.CompilerParams(
-            collective_id=0, has_side_effects=True, vmem_limit_bytes=40 * 1024 * 1024
+            collective_id=0, has_side_effects=True, vmem_limit_bytes=48 * 1024 * 1024
         ),
         name="front",
-    )(tokens, enc_up, enc_down, enc_gain.reshape(1, -1), proj_weight, selector, reorder, rows)
+    )(tokens, enc_up, enc_down, proj_weight, enc_gain.reshape(1, -1), selector, reorder, rows)
 
 
 def project_kernel(

time: 243 us -> 224 us (0.922)
  Pallas kernels: 209 us -> 199 us
  local copies, waits for them, and re-layouts: 19.7 us -> 10.6 us
    unnamed x33 -> x21, local copies, waits for them, and re-layouts: 14.2 us -> 6.03 us
    pallas_call x1, Pallas kernels: 147 us -> 140 us  [front(): pl.pallas_call(functools.partial(front_kernel, n, enc_n, req_n), out_shap...]
    pallas_call x1, Pallas kernels: 47.6 us -> 45 us  [back(): pl.pallas_call(functools.partial(back_kernel, n, room), out_shape=jax.Sha...]
  transfers between devices with their start and end apart: 1 -> 1, of which waited for: 1 -> 1; matrix products, arithmetic and copies ran while one was open for 2% -> 1% of each run, Pallas kernels for 0% -> 0%
where the time goes in v4:
time: 224 us; the launch traced here: 223 us
  Pallas kernels  199 us (89%)
  local copies, waits for them, and re-layouts  10.6 us (5%)
  matrix products  3.83 us (2%)
  starting transfers between devices  3.54 us (2%)
  other arithmetic  3.29 us (1%)
  waiting for transfers between devices  3.18 us (1%)
    pallas_call x1, Pallas kernels, front(): pl.pallas_call(functools.partial(front_kernel, n, enc_n, req_n), out_shap...  140 us
    pallas_call x1, Pallas kernels, back(): pl.pallas_call(functools.partial(back_kernel, n, room), out_shape=jax.Sha...  45 us
    pallas_call x1, Pallas kernels, project(): pl.pallas_call(functools.partial(project_kernel, q_columns // HD), grid=(...  14.2 us
    unnamed x21, local copies, waits for them, and re-layouts  6.03 us
  transfers between devices with their start and end apart: 1, of which 1 were waited for; matrix products, arithmetic and copies ran while one was open for 1% of the time, Pallas kernels for 0%

profile of v4, /device:TPU:0, one launch (start us, length us, event | category | flops | bytes accessed | tf_op | source)
XLA Modules:
  0.0 223.4 jit_solution(4509486894816217205)
XLA Ops:
  0.1 0.5 broadcast.320
  0.6 1.3 reduce.7
  2.0 0.2 convert_reduce_fusion
  2.8 0.7 fusion.21
  3.5 0.2 pad_maximum_fusion.1
  3.7 1.6 copy-done.1
  5.3 1.6 copy-done.2
  6.9 139.5 %front.1 = (bf16[4,8,32,2048]{3,2,1,0:T(8,128)(2,1)}, bf16[4,64,2048]{2,1,0:T(8,128)(2,1)S(1)}) custom-call(bf16[1024,1024]{1,0:T(8,128)(2,1)S(1)} %copy-done.1, bf16[1024,1024]{1,0:T(8,128)(2,1)S(1)} %copy-done.2, bf16[1024,1024]{1,0:T(8,128)(2,1)} %down_hbm.1, bf16[1024,2048]{1,0:T(8,128)(2,1)} %proj_hbm.1, f32[1,1024]{1,0:T(1,128)S(1)} %bitcast.67, ...), custom_call_target="tpu_custom_call" | custom-call | tf_op jit(solution)/shard_map/front/pallas_call | solution.py:340
  146.4 14.2 %project.1 = (bf16[320,1024]{1,0:T(8,128)(2,1)S(1)}, bf16[320,256]{1,0:T(8,128)(2,1)S(1)}) custom-call(f32[4,1,2048]{2,1,0:T(1,128)S(1)} %bitcast.66, bf16[4,256,2048]{2,1,0:T(8,128)(2,1)} %bitcast.70, bf16[4,64,2048]{2,1,0:T(8,128)(2,1)S(1)} %get-tuple-element.10.span_rows, bf16[8192,1024]{1,0:T(8,128)(2,1)} %q_weight.1, bf16[8192,128]{1,0:T(8,128)(2,1)S(1)} %copy-done, ...), custom_call_target="tpu_custom_call" | custom-call | tf_op jit(solution)/shard_map/project/pallas_call | solution.py:446
  160.6 0.2 reshape.253
  160.8 0.9 copy.29
  161.7 3.5 %all-to-all-start = ((bf16[4,320,64]{1,2,0:T(8,128)(2,1)}), bf16[4,320,64]{1,2,0:T(8,128)(2,1)S(1)}, u32[]{:S(2)}, u32[]{:S(2)}) async-start(bf16[4,320,64]{1,2,0:T(8,128)(2,1)} %copy.29), calls=%async_computation | async-start | bytes 393216 | tf_op jit(solution)/shard_map/all_to_all | solution.py:765
  165.4 1.3 slice.52
  166.8 0.9 copy.32
  168.0 0.1 pad_maximum_fusion
  168.1 3.2 %all-to-all-done = bf16[4,320,64]{1,2,0:T(8,128)(2,1)S(1)} async-done(((bf16[4,320,64]{1,2,0:T(8,128)(2,1)}), bf16[4,320,64]{1,2,0:T(8,128)(2,1)S(1)}, u32[]{:S(2)}, u32[]{:S(2)}) %all-to-all-start) | async-done | bytes 163872 | tf_op jit(solution)/shard_map/all_to_all | solution.py:765
  171.3 0.4 reshape.254
  172.1 0.1 copy.43
  172.2 0.2 fusion.16
  172.4 0.5 copy-done.5
  172.9 2.1 fusion.49
  175.0 1.7 fusion.5
  177.1 45.0 %back.1 = bf16[8,64,2048]{2,1,0:T(8,128)(2,1)S(1)} custom-call(bf16[320,1024]{1,0:T(8,128)(2,1)S(1)} %bitcast.65, bf16[4096,2048]{1,0:T(8,128)(2,1)} %o_weight.1, bf16[320,2048]{1,0:T(8,128)(2,1)S(1)} %bitcast.64, f32[320,128]{1,0:T(8,128)S(1)} %broadcast_in_dim.21.live_rows), custom_call_target="tpu_custom_call" | custom-call | tf_op jit(solution)/shard_map/back/pallas_call | solution.py:610
  222.1 1.3 copy.51
  (51 shorter events, 1.8 us)
Async XLA Ops:
  0.0 3.7 %copy-start.4 = (f32[1024]{0:T(1024)S(1)}, f32[1024]{0:T(1024)}, u32[]{:S(2)}) copy-start(f32[1024]{0:T(1024)} %param.19) | copy-start | bytes 12292
  3.7 1.6 copy-start.1
  5.3 1.6 copy-start.2
  6.9 139.5 %copy-start = (bf16[8192,128]{1,0:T(8,128)(2,1)S(1)}, bf16[8192,128]{1,0:T(8,128)(2,1)}, u32[]{:S(2)}) copy-start(bf16[8192,128]{1,0:T(8,128)(2,1)} %k_weight.1) | copy-start | bytes 6291460
  6.9 139.5 %copy-start.3 = (f32[8192]{0:T(1024)S(1)}, f32[8192]{0:T(1024)}, u32[]{:S(2)}) copy-start(f32[8192]{0:T(1024)} %param.21) | copy-start | bytes 98308
  161.7 9.6 %all-to-all-start = ((bf16[4,320,64]{1,2,0:T(8,128)(2,1)}), bf16[4,320,64]{1,2,0:T(8,128)(2,1)S(1)}, u32[]{:S(2)}, u32[]{:S(2)}) async-start(bf16[4,320,64]{1,2,0:T(8,128)(2,1)} %copy.29), calls=%async_computation | async-start | bytes 393216 | tf_op jit(solution)/shard_map/all_to_all | solution.py:765
  166.7 1.0 copy-start.6
  171.9 1.0 copy-start.5

commit v5 on v4

--- a/solution.py
+++ b/solution.py
@@ -208,13 +208,12 @@
     own_tokens = tokens[pl.ds(pl.multiple_of(me * share, share), share), :]
     own_sum[...] = term(me) + own_tokens.astype(jnp.float32)
 
+    for slot in range(n - 1):
+        sum_copy(slot).wait_recv()
+        own_sum[...] += partial_in[slot].astype(jnp.float32)
     if n > 2:
         arrive_step(0)
         send_step(1)
-
-    for slot in range(n - 1):
-        sum_copy(slot).wait_recv()
-        own_sum[...] += partial_in[slot].astype(jnp.float32)
     summed = own_sum[...]
     center = summed - jnp.mean(summed, axis=-1, keepdims=True)
     spread = jnp.mean(center * center, axis=-1, keepdims=True)
@@ -234,9 +233,6 @@
 
     for slot in range(n - 1):
         pool_copy(slot).start()
-    if n > 3:
-        arrive_step(1)
-        send_step(2)
     for slot in range(n - 1):
         source = lax.rem(me + n - 1 - slot, n)
         copy_to(
@@ -300,7 +296,7 @@
     for slot in range(n - 1):
         span_copy(slot).start()
 
-    for step in range(3, n - 1):
+    for step in range(2, n - 1):
         arrive_step(step - 1)
         send_step(step)
     arrive_step(n - 2)

time: 224 us -> 233 us (1.040)
  Pallas kernels: 199 us -> 207 us
    pallas_call x1, Pallas kernels: 140 us -> 145 us  [front(): pl.pallas_call(functools.partial(front_kernel, n, enc_n, req_n), out_shap...]
where the time goes in v5:
time: 233 us
  Pallas kernels  207 us (89%)
  local copies, waits for them, and re-layouts  10.6 us (5%)
  waiting for transfers between devices  4.54 us (2%)
  matrix products  3.82 us (2%)
  starting transfers between devices  3.54 us (2%)
  other arithmetic  3.29 us (1%)
    pallas_call x1, Pallas kernels, front(): pl.pallas_call(functools.partial(front_kernel, n, enc_n, req_n), out_shap...  145 us
    pallas_call x1, Pallas kernels, back(): pl.pallas_call(functools.partial(back_kernel, n, room), out_shape=jax.Sha...  46.9 us
    pallas_call x1, Pallas kernels, project(): pl.pallas_call(functools.partial(project_kernel, q_columns // HD), grid=(...  14.2 us
    unnamed x21, local copies, waits for them, and re-layouts  6.03 us
  transfers between devices with their start and end apart: 1, of which 1 were waited for; matrix products, arithmetic and copies ran while one was open for 1% of the time, Pallas kernels for 0%

profile of v5, /device:TPU:0, one launch (start us, length us, event | category | flops | bytes accessed | tf_op | source)
XLA Modules:
  0.0 232.6 jit_solution(16870640185369018227)
XLA Ops:
  0.1 0.5 broadcast.320
  0.6 1.3 reduce.7
  2.0 0.2 convert_reduce_fusion
  2.8 0.7 fusion.21
  3.5 0.2 pad_maximum_fusion.1
  3.7 1.6 copy-done.1
  5.3 1.6 copy-done.2
  6.9 145.5 %front.1 = (bf16[4,8,32,2048]{3,2,1,0:T(8,128)(2,1)}, bf16[4,64,2048]{2,1,0:T(8,128)(2,1)S(1)}) custom-call(bf16[1024,1024]{1,0:T(8,128)(2,1)S(1)} %copy-done.1, bf16[1024,1024]{1,0:T(8,128)(2,1)S(1)} %copy-done.2, bf16[1024,1024]{1,0:T(8,128)(2,1)} %down_hbm.1, bf16[1024,2048]{1,0:T(8,128)(2,1)} %proj_hbm.1, f32[1,1024]{1,0:T(1,128)S(1)} %bitcast.67, ...), custom_call_target="tpu_custom_call" | custom-call | tf_op jit(solution)/shard_map/front/pallas_call | solution.py:336
  152.4 14.2 %project.1 = (bf16[320,1024]{1,0:T(8,128)(2,1)S(1)}, bf16[320,256]{1,0:T(8,128)(2,1)S(1)}) custom-call(f32[4,1,2048]{2,1,0:T(1,128)S(1)} %bitcast.66, bf16[4,256,2048]{2,1,0:T(8,128)(2,1)} %bitcast.70, bf16[4,64,2048]{2,1,0:T(8,128)(2,1)S(1)} %get-tuple-element.10.span_rows, bf16[8192,1024]{1,0:T(8,128)(2,1)} %q_weight.1, bf16[8192,128]{1,0:T(8,128)(2,1)S(1)} %copy-done, ...), custom_call_target="tpu_custom_call" | custom-call | tf_op jit(solution)/shard_map/project/pallas_call | solution.py:442
  166.6 0.2 reshape.253
  166.8 0.9 copy.29
  167.7 3.5 %all-to-all-start = ((bf16[4,320,64]{1,2,0:T(8,128)(2,1)}), bf16[4,320,64]{1,2,0:T(8,128)(2,1)S(1)}, u32[]{:S(2)}, u32[]{:S(2)}) async-start(bf16[4,320,64]{1,2,0:T(8,128)(2,1)} %copy.29), calls=%async_computation | async-start | bytes 393216 | tf_op jit(solution)/shard_map/all_to_all | solution.py:761
  171.3 1.3 slice.52
  172.7 0.9 copy.32
  173.9 0.1 pad_maximum_fusion
  174.1 4.5 %all-to-all-done = bf16[4,320,64]{1,2,0:T(8,128)(2,1)S(1)} async-done(((bf16[4,320,64]{1,2,0:T(8,128)(2,1)}), bf16[4,320,64]{1,2,0:T(8,128)(2,1)S(1)}, u32[]{:S(2)}, u32[]{:S(2)}) %all-to-all-start) | async-done | bytes 163872 | tf_op jit(solution)/shard_map/all_to_all | solution.py:761
  178.6 0.4 reshape.254
  179.4 0.1 copy.43
  179.5 0.2 fusion.16
  179.7 0.5 copy-done.5
  180.2 2.1 fusion.49
  182.3 1.7 fusion.5
  184.4 46.9 %back.1 = bf16[8,64,2048]{2,1,0:T(8,128)(2,1)S(1)} custom-call(bf16[320,1024]{1,0:T(8,128)(2,1)S(1)} %bitcast.65, bf16[4096,2048]{1,0:T(8,128)(2,1)} %o_weight.1, bf16[320,2048]{1,0:T(8,128)(2,1)S(1)} %bitcast.64, f32[320,128]{1,0:T(8,128)S(1)} %broadcast_in_dim.21.live_rows), custom_call_target="tpu_custom_call" | custom-call | tf_op jit(solution)/shard_map/back/pallas_call | solution.py:606
  231.3 1.3 copy.51
  (51 shorter events, 1.8 us)
Async XLA Ops:
  0.0 3.7 %copy-start.4 = (f32[1024]{0:T(1024)S(1)}, f32[1024]{0:T(1024)}, u32[]{:S(2)}) copy-start(f32[1024]{0:T(1024)} %param.19) | copy-start | bytes 12292
  3.7 1.6 copy-start.1
  5.3 1.6 copy-start.2
  6.9 145.5 %copy-start = (bf16[8192,128]{1,0:T(8,128)(2,1)S(1)}, bf16[8192,128]{1,0:T(8,128)(2,1)}, u32[]{:S(2)}) copy-start(bf16[8192,128]{1,0:T(8,128)(2,1)} %k_weight.1) | copy-start | bytes 6291460
  6.9 145.5 %copy-start.3 = (f32[8192]{0:T(1024)S(1)}, f32[8192]{0:T(1024)}, u32[]{:S(2)}) copy-start(f32[8192]{0:T(1024)} %param.21) | copy-start | bytes 98308
  167.7 10.9 %all-to-all-start = ((bf16[4,320,64]{1,2,0:T(8,128)(2,1)}), bf16[4,320,64]{1,2,0:T(8,128)(2,1)S(1)}, u32[]{:S(2)}, u32[]{:S(2)}) async-start(bf16[4,320,64]{1,2,0:T(8,128)(2,1)} %copy.29), calls=%async_computation | async-start | bytes 393216 | tf_op jit(solution)/shard_map/all_to_all | solution.py:761
  172.6 1.0 copy-start.6
  179.2 1.0 copy-start.5
